TPU v7x, 32 devices: a whole 2x2x4 slice. The times are simulated.
32 devices in a mesh: ctx: 16 (over z, y, x), tp: 2 (over core).
Axes of the slice: x: 2, y: 2, z: 4, core: 2. Of those that a mesh axis runs over, the one named last changes fastest.
Arguments:
- queries: bfloat16 [2048, 4096], P('ctx', 'tp'), may hold values from -16 to 16
- keys: bfloat16 [2048, 1024], P('ctx', 'tp'), may hold values from -7.1 to 7.1
- values: bfloat16 [2048, 1024], P('ctx', 'tp'), may hold values from -6 to 6
- mixer_input: bfloat16 [2048, 8192], P('ctx', 'tp'), may hold values from -6 to 6
- gate: bfloat16 [2048, 8192], P('ctx', 'tp'), may hold values from -6 to 6
- step_weight: bfloat16 [8192, 128], P('tp'), may hold values from -0.0625 to 0.0625
- state_weight: bfloat16 [8192, 32], P('tp'), may hold values from -0.0625 to 0.0625
- step_bias: float32 [128], P('tp'), may hold values from -1 to 1
- decay_rate: float32 [128], P('tp'), may hold values from 4.8828124e-06 to 0.05
- skip_gain: float32 [128], P('tp'), may hold values from 0.5 to 2
- norm_gain: float32 [8192], P('tp'), may hold values from 0.1 to 1.9
Outputs:
- attention_out: bfloat16 [2048, 4096], P('ctx', 'tp')
- mamba_out: bfloat16 [2048, 8192], P('ctx', 'tp')
All inputs are finite; a program needn't handle non-finite values.
Results may differ from a plain program's by a relative error of at most 0.0044.
Values may be sent and summed in bfloat16 or wider, within the bound.
No kernel may reach another device: no remote copies, remote signals or barrier semaphores. Data moves between devices by JAX's collectives and lax.ppermute only.
A program may use at most 64 MiB of HBM per device.

v0:
```python
import functools
import math

import jax
import jax.numpy as jnp
from jax import lax
from jax.experimental import pallas as pl
from jax.experimental.pallas import tpu as pltpu
from jax.sharding import PartitionSpec as P

HD = 128
DECAY_CHANNELS = 64
SCAN_TOKENS = 128
LANES = 128
UNROLL = 8
LOG2E = math.log2(math.e)
VMEM_LIMIT = 14 * 1024 * 1024

F32 = jnp.float32
BF16 = jnp.bfloat16


def vmem():
    return pl.BlockSpec(memory_space=pltpu.VMEM)


def hbm():
    return pl.BlockSpec(memory_space=pltpu.HBM)


def launch(kernel, name, out_shape, *inputs, after=(), flops=0, scratch=(), in_specs=None, out_specs=None, grid=None):
    count, skip = len(inputs), len(after)
    single = isinstance(out_shape, jax.ShapeDtypeStruct)
    shapes = [out_shape] if single else list(out_shape)
    size = sum(x.size * x.dtype.itemsize for x in list(inputs) + shapes)

    def body(*refs):
        kernel(*refs[:count], *refs[count + skip :])

    result = pl.pallas_call(
        body,
        **({} if grid is None else {"grid": grid}),
        out_shape=shapes,
        in_specs=(in_specs or [vmem()] * count) + [pl.BlockSpec(memory_space=pl.ANY)] * skip,
        out_specs=out_specs or [vmem()] * len(shapes),
        scratch_shapes=list(scratch),
        compiler_params=pltpu.CompilerParams(vmem_limit_bytes=VMEM_LIMIT),
        cost_estimate=pl.CostEstimate(flops=flops, bytes_accessed=size, transcendentals=0),
        name=name,
    )(*inputs, *after)
    return result[0] if single else result


def place(group):
    return lax.rem(lax.axis_index("ctx"), jnp.int32(group))


def swap(pieces, group, count):
    result = list(pieces)
    for k in reversed(range(1, group)):
        perm = [(i, (i // group) * group + ((i % group) ^ k)) for i in range(count)]
        result[k] = lax.ppermute(pieces[k], "ctx", perm)
    return result


def climb_up(array, group, count, steps=1, first=0):
    perm = [(i, i + group * steps) for i in range(group * first, count - group * steps)]
    return lax.ppermute(array, "ctx", perm)


def shape_of(shape, dtype):
    return jax.ShapeDtypeStruct(shape, dtype)


def tie(array, after):
    return pl.pallas_call(
        lambda *refs: None,
        out_shape=shape_of(array.shape, array.dtype),
        in_specs=[pl.BlockSpec(memory_space=pl.ANY)] * (1 + len(after)),
        out_specs=pl.BlockSpec(memory_space=pl.ANY),
        input_output_aliases={0: 0},
        compiler_params=pltpu.CompilerParams(vmem_limit_bytes=1024 * 1024),
        name="tie",
    )(array, *after)


def pack_kv(keys, values, group):
    length, width = keys.shape
    piece = width // group

    def kernel(k_ref, v_ref, *outs):
        mine = place(group)
        for k in range(group):
            columns = pl.ds(pl.multiple_of((mine ^ k) * piece, piece), piece)
            outs[k][0] = k_ref[:, columns]
            outs[k][1] = v_ref[:, columns]

    return launch(
        kernel,
        "pack_kv",
        [shape_of((2, length, piece), keys.dtype)] * group,
        keys,
        values,
        flops=5000000000,
        grid=(1,),
        in_specs=[pl.BlockSpec((length, width), lambda i: (0, 0))] * 2,
    )


def join(pieces, group):
    length, width = pieces[0].shape

    def kernel(*refs):
        out_ref, sems = refs[group:]
        mine = place(group)
        copies = []
        for k in range(group):
            columns = pl.ds(pl.multiple_of((mine ^ k) * width, width), width)
            copies.append(
                pltpu.make_async_copy(refs[group - 1 - k], out_ref.at[:, columns], sems.at[k])
            )
        for copy in copies:
            copy.start()
        for copy in copies:
            copy.wait()

    return launch(
        kernel,
        "join_heads",
        shape_of((length, width * group), pieces[0].dtype),
        *reversed(pieces),
        out_specs=[hbm()],
        scratch=[pltpu.SemaphoreType.DMA((group,))],
    )


def flash_chunk(q_refs, kv_ref, before, after, extended, own, length):
    group = len(q_refs)
    heads = q_refs[0].shape[1] // HD
    kv_heads = kv_ref.shape[3] // HD
    share = heads // kv_heads
    rows = group * length
    tile = min(rows, 2 * length)
    rate = LOG2E / math.sqrt(HD)
    for kv in range(kv_heads):
        lanes = slice(kv * HD, (kv + 1) * HD)
        keys = kv_ref[:, 0, :, lanes].reshape(rows, HD)
        extended[:, :HD] = kv_ref[:, 1, :, lanes].reshape(rows, HD)
        extended[:, HD:] = jnp.ones((rows, HD), BF16)
        tiles = [
            (h, start)
            for start in range(0, rows, tile)
            for h in range(kv * share, (kv + 1) * share)
        ]

        def score(h, start):
            parts = q_refs[start // length : (start + tile) // length]
            q = [ref[:length, h * HD : (h + 1) * HD] for ref in parts]
            q = jnp.concatenate(q, axis=0) if len(q) > 1 else q[0]
            scores = lax.dot_general(
                q, keys, (((1,), (1,)), ((), ())), preferred_element_type=F32
            )
            if own:
                flip = place(group) * length
                row = (lax.broadcasted_iota(jnp.int32, (tile, rows), 0) + start) ^ flip
                column = lax.broadcasted_iota(jnp.int32, (tile, rows), 1) ^ flip
                scores = jnp.where(column <= row, scores, -1e30)
            return scores

        ahead = score(*tiles[0])
        for n, (h, start) in enumerate(tiles):
            scores = ahead
            if n + 1 < len(tiles):
                ahead = score(*tiles[n + 1])
            here = slice(start, start + tile)
            top = jnp.broadcast_to(jnp.max(scores, axis=1, keepdims=True), (tile, LANES))
            if not own:
                top_before = before[1][h, here]
                top = jnp.maximum(top_before, top)
            across = [top] * (rows // LANES)
            across = jnp.concatenate(across, axis=1) if len(across) > 1 else top
            weights = jnp.exp2((scores - across) * rate).astype(BF16)
            value = jnp.dot(weights, extended[...], preferred_element_type=F32)
            if not own:
                keep = jnp.exp2((top_before - top) * rate)
                value = value + before[0][h, here] * jnp.concatenate([keep, keep], axis=1)
            yield h, start, tile, value
            if after is not None:
                after[0][h, here] = value
                after[1][h, here] = top


def finish_rows(out_refs, h, start, tile, value):
    length = out_refs[0].shape[0]
    result = (value[:, :HD] / value[:, HD:]).astype(BF16)
    for at in range(0, tile, length):
        out_refs[(start + at) // length][:, h * HD : (h + 1) * HD] = result[at : at + length]


def flash(q, length, own=None, state=(), chunks=(), final=False, base=1, after=()):
    group = len(q)
    heads = q[0].shape[1] // HD
    rows = group * length
    fixed = isinstance(base, int)
    has_own = own is not None
    specs = [] if fixed else [pl.BlockSpec(memory_space=pltpu.SMEM)]
    rest = list(q) + ([own] if has_own else []) + list(state) + list(chunks)
    specs = specs + [vmem()] * len(rest)

    def kernel(*refs):
        refs = list(refs)
        first = base if fixed else refs.pop(0)[0]
        q_refs = [refs.pop(0) for _ in range(group)]
        own_ref = refs.pop(0) if has_own else None
        held = None if has_own else (refs.pop(0), refs.pop(0))
        chunk_refs = [refs.pop(0) for _ in range(len(chunks))]
        extended = refs.pop()
        turn = lax.axis_index("ctx") // group
        outs = None if final else tuple(refs)
        if has_own:
            for done in flash_chunk(q_refs, own_ref, None, outs, extended, True, length):
                if final:
                    finish_rows(refs, *done)
            held = outs
        for number, ref in enumerate(chunk_refs):

            @pl.when(turn >= first + number)
            def _(ref=ref, held=held):
                for done in flash_chunk(q_refs, ref, held, outs, extended, False, length):
                    if final:
                        finish_rows(refs, *done)

            if not has_own and number == 0:

                @pl.when(turn < first)
                def _(held=held):
                    for h in range(heads):
                        if final:
                            finish_rows(refs, h, 0, rows, held[0][h])
                        else:
                            outs[0][h] = held[0][h]
                            outs[1][h] = held[1][h]

            held = outs

    if final:
        out_shape = [shape_of((length, heads * HD), BF16)] * group
    else:
        out_shape = [
            shape_of((heads, rows, HD + LANES), F32),
            shape_of((heads, rows, LANES), F32),
        ]
    parts = len(chunks) + has_own
    return launch(
        kernel,
        "flash",
        out_shape,
        *([] if fixed else [base]),
        *rest,
        after=after,
        in_specs=specs,
        flops=4 * heads * rows * rows * HD * parts,
        scratch=[pltpu.VMEM((rows, HD + LANES), BF16)],
    )


def widen(row, lanes):
    extra = lanes - row.shape[1]
    if not extra:
        return row
    return jnp.concatenate([row, jnp.zeros((row.shape[0], extra), row.dtype)], axis=1)


def project(x, step_weight, state_weight, after=()):
    length, channels = x.shape
    heads = step_weight.shape[1]

    def kernel(x_ref, step_ref, map_ref, out_ref):
        x = x_ref[...]
        out_ref[:, :heads] = jnp.dot(x, step_ref[...], preferred_element_type=F32)
        maps = lax.dot_general(
            x, map_ref[...], (((1,), (1,)), ((), ())), preferred_element_type=F32
        )
        out_ref[:, heads:] = widen(maps, LANES)

    return launch(
        kernel,
        "project",
        shape_of((length, heads + LANES), F32),
        x,
        step_weight,
        state_weight.T,
        after=after,
        flops=4 * length * channels * heads,
    )


def owners(heads):
    shape = (LANES, heads * DECAY_CHANNELS)
    head = lax.broadcasted_iota(jnp.int32, shape, 0)
    channel = lax.broadcasted_iota(jnp.int32, shape, 1)
    return (channel // DECAY_CHANNELS == head).astype(BF16)


def pack_row(row, rows):
    high = row.astype(BF16).astype(F32)
    rest = row - high
    middle = rest.astype(BF16).astype(F32)
    low = rest - middle
    return jnp.concatenate([high, middle, low, jnp.zeros((rows - 3, row.shape[1]), F32)], axis=0)


def unpack_row(rows):
    rows = rows.astype(F32)
    return rows[0:1] + rows[1:2] + rows[2:3]


def spread_total(rows, owner):
    wide = jnp.dot(rows, owner, preferred_element_type=F32)
    return wide[0:1] + wide[1:2] + wide[2:3]


def block_state(parts, bias, rate, x, q, states, group, after=()):
    length, channels = x.shape
    every = parts[0].shape[1] - LANES
    heads = bias.shape[1]
    width = channels // group
    columns = q.shape[1] // group
    bands = width // columns
    count = len(parts)

    def kernel(*refs):
        bias_ref, rate_ref, x_ref, q_ref = refs[count : count + 4]
        climb_ref, climb_t_ref, step_t_ref, maps_ref = refs[count + 4 : count + 8]
        outs = refs[count + 8 : count + 8 + group]
        held = refs[count + 8 + group]
        summed = refs[0][...]
        for ref in refs[1:count]:
            summed = summed + ref[...]
        shift = lax.rem(every - lax.axis_index("tp") * heads, jnp.int32(every))
        raw = pltpu.roll(summed[:, :every], shift, 1) + widen(bias_ref[...], every)
        step = jnp.maximum(raw, 0.0) + jnp.log1p(jnp.exp(-jnp.abs(raw)))
        log_decay = -widen(rate_ref[...], every) * step
        row = lax.broadcasted_iota(jnp.int32, (length, length), 0)
        column = lax.broadcasted_iota(jnp.int32, (length, length), 1)
        lower = (column <= row).astype(F32)
        climb = jnp.dot(
            lower, log_decay, precision=lax.Precision.HIGHEST, preferred_element_type=F32
        )
        maps = summed[:, every:]
        climb_ref[...] = climb * LOG2E
        maps_ref[...] = maps
        climb_t = climb.T
        step_t = step.T
        climb_t_ref[...] = climb_t[:heads] * LOG2E
        step_t_ref[...] = step_t[:heads]
        b_t = maps.T[:states]
        weight_t = jnp.exp(climb_t[:, length - 1 :] - climb_t) * step_t
        bundle = 4
        span = bundle * DECAY_CHANNELS
        owner = lax.broadcasted_iota(jnp.int32, (1, span), 1) // DECAY_CHANNELS
        for at in range(0, heads, bundle):
            feed = [b_t * weight_t[at + i : at + i + 1] for i in range(bundle)]
            feed = jnp.concatenate(feed, axis=0).astype(BF16)
            start = at * DECAY_CHANNELS
            product = jnp.dot(feed, x_ref[:, start : start + span], preferred_element_type=F32)
            state = product[:states]
            for i in range(1, bundle):
                state = jnp.where(owner == i, product[i * states : (i + 1) * states], state)
            piece, offset = divmod(start, width)
            band, offset = divmod(offset, columns)
            rows = slice(band * states, (band + 1) * states)
            held[piece, rows, offset : offset + span] = state.astype(BF16)
        totals = pack_row(climb[length - 1 :], states)
        for piece in range(group):
            at = piece * (heads // group)
            here = totals if not at else pltpu.roll(totals, every - at, 1)
            held[piece, bands * states :, :] = widen(here[:, :LANES], columns).astype(BF16)
        mine = place(group)
        for k in range(group):
            here = pl.ds(pl.multiple_of((mine ^ k) * columns, columns), columns)
            outs[k][:length] = q_ref[:, here]
            outs[k][length:] = held[mine ^ k]

    payload = shape_of((length + (bands + 1) * states, columns), BF16)
    result = launch(
        kernel,
        "block_state",
        [
            shape_of((length, every), F32),
            shape_of((heads, length), F32),
            shape_of((heads, length), F32),
            shape_of((length, LANES), F32),
        ]
        + [payload] * group,
        *parts,
        bias,
        rate,
        x,
        q,
        after=after,
        flops=32 * length * states * channels,
        scratch=[pltpu.VMEM((group, (bands + 1) * states, columns), BF16)],
    )
    return result[:4], result[4:]


def local_part(x, gate, climb, climb_t, step_t, maps, skip, states, after=()):
    length, channels = x.shape
    heads = channels // DECAY_CHANNELS

    def kernel(
        x_ref, gate_ref, climb_ref, climb_t_ref, step_t_ref, maps_ref, skip_ref, still_ref, scale_ref
    ):
        maps = maps_ref[...]
        inner = lax.dot_general(
            maps[:, states : 2 * states],
            maps[:, :states],
            (((1,), (1,)), ((), ())),
            precision=lax.Precision.HIGHEST,
            preferred_element_type=F32,
        )
        row = lax.broadcasted_iota(jnp.int32, (length, length), 0)
        column = lax.broadcasted_iota(jnp.int32, (length, length), 1)
        inner = jnp.where(column <= row, inner, 0.0)
        left = lax.broadcasted_iota(jnp.int32, (length, LANES), 1) < DECAY_CHANNELS

        for j in range(0, heads, 2):
            columns = slice(j * DECAY_CHANNELS, j * DECAY_CHANNELS + LANES)
            x = x_ref[:, columns]
            wide = [jnp.broadcast_to(climb_ref[:, i : i + 1], (length, length)) for i in (j, j + 1)]
            mixed = []
            for i in (j, j + 1):
                fall = jnp.minimum(wide[i - j] - climb_t_ref[i : i + 1], 0.0)
                mixed.append((inner * jnp.exp2(fall) * step_t_ref[i : i + 1]).astype(BF16))
            zero = jnp.zeros_like(x)
            feeds = jnp.concatenate([jnp.where(left, x, zero), jnp.where(left, zero, x)], axis=0)
            local = jnp.dot(jnp.concatenate(mixed, axis=1), feeds, preferred_element_type=F32)
            gain = jnp.where(left[:1], skip_ref[:, j : j + 1], skip_ref[:, j + 1 : j + 2])
            grown = jnp.exp2(jnp.where(left, wide[0], wide[1]))
            gate = gate_ref[:, columns].astype(F32)
            half = 0.5 * gate
            silu = half + half * jnp.tanh(half)
            still_ref[:, columns] = (local + gain * x.astype(F32)) * silu
            scale_ref[:, columns] = grown * silu

    return launch(
        kernel,
        "local_part",
        [shape_of((length, channels), F32)] * 2,
        x,
        gate,
        climb,
        climb_t,
        step_t,
        maps,
        skip,
        after=after,
        flops=4 * length * length * channels,
    )


def gather_blocks(group, states, length, refs, held):
    mine = place(group)
    for k in range(group):
        held[mine ^ k] = refs[k][length:]


def block_of(held, b, states, columns, width):
    bands = width // columns
    rows = [held[b, i * states : (i + 1) * states] for i in range(bands)]
    state = jnp.concatenate(rows, axis=1) if bands > 1 else rows[0]
    return state.astype(F32), held[b, bands * states :, :LANES]


def group_total(payloads, length, states, width, after=()):
    group = len(payloads)
    rows, columns = payloads[0].shape
    heads = width // DECAY_CHANNELS

    def kernel(*refs):
        out_ref, held = refs[group:]
        gather_blocks(group, states, length, refs[:group], held)
        owner = owners(heads)
        state, packed = block_of(held, 0, states, columns, width)
        total = unpack_row(packed)
        for b in range(1, group):
            more, packed = block_of(held, b, states, columns, width)
            state = jnp.exp(spread_total(packed, owner)) * state + more
            total = total + unpack_row(packed)
        out_ref[:, :width] = state.astype(BF16)
        out_ref[:, width:] = pack_row(total, states).astype(BF16)

    return launch(
        kernel,
        "group_total",
        shape_of((states, width + LANES), BF16),
        *payloads,
        after=after,
        scratch=[pltpu.VMEM((group, rows - length, columns), BF16)],
    )


def entering_states(payloads, earlier, length, states, width, after=()):
    group = len(payloads)
    rows, columns = payloads[0].shape
    heads = width // DECAY_CHANNELS
    count = len(earlier)

    def kernel(*refs):
        earlier_refs = refs[group : group + count]
        outs = refs[group + count : 2 * group + count]
        held, entering = refs[2 * group + count :]
        gather_blocks(group, states, length, refs[:group], held)
        owner = owners(heads)
        state = jnp.zeros((states, width), F32)
        for ref in reversed(earlier_refs):
            state = jnp.exp(spread_total(ref[:, width:], owner)) * state
            state = state + ref[:, :width].astype(F32)
        for b in range(group):
            entering[b] = state
            if b < group - 1:
                more, packed = block_of(held, b, states, columns, width)
                state = jnp.exp(spread_total(packed, owner)) * state + more
        mine = place(group)
        for k in range(group):
            outs[k][...] = entering[mine ^ k]

    return launch(
        kernel,
        "entering_states",
        [shape_of((states, width), F32)] * group,
        *payloads,
        *earlier,
        after=after,
        scratch=[
            pltpu.VMEM((group, rows - length, columns), BF16),
            pltpu.VMEM((group, states, width), F32),
        ],
    )


def carried_part(maps, still, scale, entering, states, after=()):
    length, channels = still.shape
    group = len(entering)
    width = channels // group
    span = min(width, 512)

    def kernel(maps_ref, still_ref, scale_ref, *refs):
        gated_ref, square_ref, held = refs[group:]
        mine = place(group)
        for k in range(group):
            held[mine ^ k] = refs[k][...]
        c = maps_ref[:, states : 2 * states]
        c_high = c.astype(BF16)
        c_low = (c - c_high.astype(F32)).astype(BF16)
        c = jnp.concatenate([c_high, c_low, c_high], axis=1)
        folded = jnp.zeros(square_ref.shape, F32)
        for at in range(0, channels, span):
            piece, offset = divmod(at, width)
            state = held[piece, :, offset : offset + span]
            high = state.astype(BF16)
            low = (state - high.astype(F32)).astype(BF16)
            carried = jnp.dot(
                c, jnp.concatenate([high, high, low], axis=0), preferred_element_type=F32
            )
            columns = slice(at, at + span)
            gated = still_ref[:, columns] + scale_ref[:, columns] * carried
            gated_ref[:, columns] = gated
            square = gated * gated
            for lane in range(0, span, LANES):
                folded = folded + square[:, lane : lane + LANES]
        square_ref[...] = folded

    return launch(
        kernel,
        "carried_part",
        [shape_of((length, channels), F32), shape_of((length, LANES), F32)],
        maps,
        still,
        scale,
        *entering,
        after=after,
        flops=6 * length * states * channels,
        scratch=[pltpu.VMEM((group, states, width), F32)],
    )


def norm(gated, gain, squares, every):
    length, channels = gated.shape
    count = len(squares)

    def kernel(gated_ref, gain_ref, *refs):
        out_ref = refs[count]
        square = refs[0][...]
        for ref in refs[1:count]:
            square = square + ref[...]
        mean = jnp.sum(square, axis=1, keepdims=True) / every
        factor = jnp.broadcast_to(lax.rsqrt(mean + 1e-05), square.shape)
        for at in range(0, channels, LANES):
            columns = slice(at, at + LANES)
            out_ref[:, columns] = (gated_ref[:, columns] * factor * gain_ref[:, columns]).astype(BF16)

    return launch(
        kernel, "norm", shape_of((length, channels), BF16), gated, gain, *squares
    )


def shared_parts(part):
    if lax.axis_size("tp") == 2:
        return [part, lax.ppermute(part, "tp", [(0, 1), (1, 0)])]
    return [lax.psum(part, "tp")]


def earlier_states(total, group, turns, count, states, width):
    if turns <= UNROLL:
        return [climb_up(total, group, count, steps) for steps in range(1, turns)]
    heads = width // DECAY_CHANNELS

    def one(_, carry):
        travelling, summed, ahead = carry
        travelling = climb_up(travelling, group, count)
        summed = summed + jnp.exp(ahead) * travelling[:, :width].astype(F32)
        more = unpack_row(travelling[:, width : width + heads])
        return travelling, summed, ahead + jnp.repeat(more, DECAY_CHANNELS, axis=1)

    start = (total, jnp.zeros((states, width), F32), jnp.zeros((1, width), F32))
    _, summed, _ = lax.fori_loop(1, turns, one, start)
    return [jnp.concatenate([summed.astype(BF16), jnp.zeros((states, LANES), BF16)], axis=1)]


def per_device(
    queries,
    keys,
    values,
    mixer_input,
    gate,
    step_weight,
    state_weight,
    step_bias,
    decay_rate,
    skip_gain,
    norm_gain,
):
    count = lax.axis_size("ctx")
    length = queries.shape[0]
    channels = mixer_input.shape[1]
    states = state_weight.shape[1] // 2
    group = math.gcd(keys.shape[1] // HD, count)
    turns = count // group
    width = channels // group

    packed = pack_kv(keys, values, group)
    parts = shared_parts(project(mixer_input, step_weight, state_weight, after=packed[:1]))
    blocks = swap(packed, group, count)
    (climb, climb_t, step_t, maps), payloads = block_state(
        parts, step_bias[None], decay_rate[None], mixer_input, queries, states, group
    )
    still, scale = local_part(
        mixer_input, gate, climb, climb_t, step_t, maps, skip_gain[None], states
    )
    own = jnp.stack([tie(blocks[0], [still])] + blocks[1:])
    sent = payloads[:1]
    payloads = swap(payloads, group, count)
    ring = 1 < turns <= UNROLL
    arrived, ready = [], []
    if ring:
        arrived.append(climb_up(own, group, count))
    if ring and turns > 2:
        arrived[0] = tie(arrived[0], sent)
        ready = [arrived[0]]
        arrived.append(climb_up(arrived[0], group, count, first=1))
    total = group_total(payloads, length, states, width, after=ready)
    earlier = earlier_states(total, group, turns, count, states, width)
    state = flash(payloads, length, own=own, chunks=arrived[:-1][:1], after=[total])
    if ring and turns > 3:
        arrived[1] = tie(arrived[1], [state[1]] + earlier[:1] + earlier[:0:-1])
        ready = [arrived[1]]
        for step in range(2, turns - 1):
            arrived.append(climb_up(arrived[-1], group, count, first=step))
    entering = entering_states(payloads, earlier, length, states, width, after=ready)
    if ring and turns > 3:
        state = flash(
            payloads, length, state=state, chunks=arrived[1:-1], base=2, after=entering[:1]
        )
    entering = swap(entering, group, count)
    if turns > 1 and not ring:

        def one(step, carry):
            chunk, state = carry
            chunk = climb_up(chunk, group, count)
            state = flash(payloads, length, state=state, chunks=[chunk], base=jnp.reshape(step, (1,)))
            return chunk, tuple(state)

        chunk, state = lax.fori_loop(1, turns - 1, one, (own, tuple(state)))
        arrived.append(climb_up(chunk, group, count))
    gated, square = carried_part(maps, still, scale, entering, states)
    mamba_out = norm(
        gated, norm_gain[None], shared_parts(square), channels * lax.axis_size("tp")
    )
    if turns == 1:
        outs = flash(payloads, length, own=own, final=True)
    else:
        outs = flash(
            payloads, length, state=state, chunks=arrived[-1:], final=True, base=turns - 1
        )
    return join(swap(outs, group, count), group), mamba_out


def solution(mesh):
    return jax.shard_map(
        per_device,
        mesh=mesh,
        in_specs=(
            P("ctx", "tp"),
            P("ctx", "tp"),
            P("ctx", "tp"),
            P("ctx", "tp"),
            P("ctx", "tp"),
            P("tp", None),
            P("tp", None),
            P("tp"),
            P("tp"),
            P("tp"),
            P("tp"),
        ),
        out_specs=(P("ctx", "tp"), P("ctx", "tp")),
        check_vma=False,
    )
```

profile of v0, /device:TPU:24, one launch (start us, length us, event | category | flops | bytes accessed | tf_op | source)
XLA Modules:
  0.0 50.6 jit_solution(13582589850380235211)
XLA Ops:
  0.7 1.0 %copy-done.9 = bf16[128,512]{1,0:T(8,128)(2,1)S(1)} copy-done((bf16[128,512]{1,0:T(8,128)(2,1)S(1)}, bf16[128,512]{1,0:T(8,128)(2,1)}, u32[]{:S(2)}) %copy-start.9) | copy-done | bytes 131096
  3.6 1.6 %collective-permute-start.4 = (bf16[2,128,128]{2,1,0:T(8,128)(2,1)S(1)}, bf16[2,128,128]{2,1,0:T(8,128)(2,1)S(1)}, u32[]{:S(2)}, u32[]{:S(2)}) collective-permute-start(bf16[2,128,128]{2,1,0:T(8,128)(2,1)S(1)} %get-tuple-element.40), channel_id=1, source_target_pairs={{0,2},{2,0},{4,6},{6,4},{8,10},{10,8},{12,14},{14,12},{16,18},{18,... | collective-permute-start | bytes 196616 | tf_op jit(solution)/shard_map/ppermute | solution.py:62
  5.1 1.5 %collective-permute-start.5 = (bf16[2,128,128]{2,1,0:T(8,128)(2,1)S(1)}, bf16[2,128,128]{2,1,0:T(8,128)(2,1)S(1)}, u32[]{:S(2)}, u32[]{:S(2)}) collective-permute-start(bf16[2,128,128]{2,1,0:T(8,128)(2,1)S(1)} %get-tuple-element.41), channel_id=1, source_target_pairs={{0,4},{2,6},{4,0},{6,2},{8,12},{10,14},{12,8},{14,10},{16,20},{18,... | collective-permute-start | bytes 196616 | tf_op jit(solution)/shard_map/ppermute | solution.py:62
  8.0 2.3 %local_part.1 = (f32[128,4096]{1,0:T(8,128)S(1)}, f32[128,4096]{1,0:T(8,128)S(1)}) custom-call(bf16[128,4096]{1,0:T(8,128)(2,1)S(1)} %copy-done, bf16[128,4096]{1,0:T(8,128)(2,1)S(1)} %copy-done.1, f32[128,128]{1,0:T(8,128)S(1)} %get-tuple-element.35.refs_2_, f32[64,128]{1,0:T(8,128)S(1)} %get-tuple-element.36.refs_3_, ...), custom_call_target="tpu_custom_call" | custom-call | flops 268435456 | bytes 6488320 | tf_op jit(solution)/shard_map/local_part/pallas_call | solution.py:40
  10.3 1.5 %collective-permute-done.6 = bf16[2,128,128]{2,1,0:T(8,128)(2,1)S(1)} collective-permute-done((bf16[2,128,128]{2,1,0:T(8,128)(2,1)S(1)}, bf16[2,128,128]{2,1,0:T(8,128)(2,1)S(1)}, u32[]{:S(2)}, u32[]{:S(2)}) %collective-permute-start.6) | collective-permute-done | bytes 65568 | tf_op jit(solution)/shard_map/ppermute | solution.py:62
  11.8 1.3 %collective-permute-start.7 = (bf16[4,2,128,128]{3,2,1,0:T(8,128)(2,1)S(1)}, bf16[4,2,128,128]{3,2,1,0:T(8,128)(2,1)S(1)}, u32[]{:S(2)}, u32[]{:S(2)}) collective-permute-start(bf16[4,2,128,128]{3,2,1,0:T(8,128)(2,1)S(1)} %pad_maximum_fusion.refs_4_), channel_id=1, source_target_pairs={{0,8},{2,10},{4,12},{6,14},{8,16},{10,18},{12,20},{14,22},{16,24},... | collective-permute-start | bytes 786440 | tf_op jit(solution)/shard_map/ppermute | solution.py:68
  13.7 1.0 %collective-permute-start.2 = (bf16[176,512]{1,0:T(8,128)(2,1)S(1)}, bf16[176,512]{1,0:T(8,128)(2,1)S(1)}, u32[]{:S(2)}, u32[]{:S(2)}) collective-permute-start(bf16[176,512]{1,0:T(8,128)(2,1)S(1)} %get-tuple-element.33), channel_id=1, source_target_pairs={{0,4},{2,6},{4,0},{6,2},{8,12},{10,14},{12,8},{14,10},{16,20},{18,... | collective-permute-start | bytes 540680 | tf_op jit(solution)/shard_map/ppermute | solution.py:62
  14.8 1.9 %collective-permute-start.3 = (bf16[176,512]{1,0:T(8,128)(2,1)S(1)}, bf16[176,512]{1,0:T(8,128)(2,1)S(1)}, u32[]{:S(2)}, u32[]{:S(2)}) collective-permute-start(bf16[176,512]{1,0:T(8,128)(2,1)S(1)} %get-tuple-element.34), channel_id=1, source_target_pairs={{0,6},{2,4},{4,2},{6,0},{8,14},{10,12},{12,10},{14,8},{16,22},{18,... | collective-permute-start | bytes 540680 | tf_op jit(solution)/shard_map/ppermute | solution.py:62
  16.7 4.0 %collective-permute-done.7.refs_0_ = bf16[4,2,128,128]{3,2,1,0:T(8,128)(2,1)S(1)} collective-permute-done((bf16[4,2,128,128]{3,2,1,0:T(8,128)(2,1)S(1)}, bf16[4,2,128,128]{3,2,1,0:T(8,128)(2,1)S(1)}, u32[]{:S(2)}, u32[]{:S(2)}) %collective-permute-start.7) | collective-permute-done | bytes 262176 | tf_op jit(solution)/shard_map/ppermute | solution.py:68
  20.7 1.3 %collective-permute-start.8 = (bf16[4,2,128,128]{3,2,1,0:T(8,128)(2,1)S(1)}, bf16[4,2,128,128]{3,2,1,0:T(8,128)(2,1)S(1)}, u32[]{:S(2)}, u32[]{:S(2)}) collective-permute-start(bf16[4,2,128,128]{3,2,1,0:T(8,128)(2,1)S(1)} %tie.4.refs_4_.refs_5_), channel_id=1, source_target_pairs={{8,16},{10,18},{12,20},{14,22},{16,24},{18,26},{20,28},{22,30},{9,... | collective-permute-start | bytes 786440 | tf_op jit(solution)/shard_map/ppermute | solution.py:68
  22.0 1.1 %collective-permute-done.2.refs_2_ = bf16[176,512]{1,0:T(8,128)(2,1)S(1)} collective-permute-done((bf16[176,512]{1,0:T(8,128)(2,1)S(1)}, bf16[176,512]{1,0:T(8,128)(2,1)S(1)}, u32[]{:S(2)}, u32[]{:S(2)}) %collective-permute-start.2) | collective-permute-done | bytes 180256 | tf_op jit(solution)/shard_map/ppermute | solution.py:62
  23.3 1.3 %collective-permute-start.10 = (bf16[16,1152]{1,0:T(8,128)(2,1)S(1)}, bf16[16,1152]{1,0:T(8,128)(2,1)S(1)}, u32[]{:S(2)}, u32[]{:S(2)}) collective-permute-start(bf16[16,1152]{1,0:T(8,128)(2,1)S(1)} %group_total.1.refs_6_), channel_id=1, source_target_pairs={{0,24},{2,26},{4,28},{6,30},{1,25},{3,27},{5,29},{7,31}} | collective-permute-start | bytes 110600 | tf_op jit(solution)/shard_map/ppermute | solution.py:68
  24.6 1.3 %collective-permute-start.11 = (bf16[16,1152]{1,0:T(8,128)(2,1)S(1)}, bf16[16,1152]{1,0:T(8,128)(2,1)S(1)}, u32[]{:S(2)}, u32[]{:S(2)}) collective-permute-start(bf16[16,1152]{1,0:T(8,128)(2,1)S(1)} %group_total.1.refs_6_), channel_id=1, source_target_pairs={{0,16},{2,18},{4,20},{6,22},{8,24},{10,26},{12,28},{14,30},{1,17},... | collective-permute-start | bytes 110600 | tf_op jit(solution)/shard_map/ppermute | solution.py:68
  25.9 1.3 %collective-permute-start.9 = (bf16[16,1152]{1,0:T(8,128)(2,1)S(1)}, bf16[16,1152]{1,0:T(8,128)(2,1)S(1)}, u32[]{:S(2)}, u32[]{:S(2)}) collective-permute-start(bf16[16,1152]{1,0:T(8,128)(2,1)S(1)} %group_total.1.refs_6_), channel_id=1, source_target_pairs={{0,8},{2,10},{4,12},{6,14},{8,16},{10,18},{12,20},{14,22},{16,24},... | collective-permute-start | bytes 110600 | tf_op jit(solution)/shard_map/ppermute | solution.py:68
  27.2 3.4 %flash.3 = (f32[4,512,256]{2,1,0:T(8,128)S(1)}, f32[4,512,128]{2,1,0:T(8,128)S(1)}) custom-call(bf16[176,512]{1,0:T(8,128)(2,1)S(1)} %get-tuple-element.31.refs_1_.refs_0_, bf16[176,512]{1,0:T(8,128)(2,1)S(1)} %collective-permute-done.1.refs_1_, bf16[176,512]{1,0:T(8,128)(2,1)S(1)} %collective-permute-done.2.refs_2_, ...), custom_call_target="tpu_custom_call" | custom-call | flops 1073741824 | bytes 4390912 | tf_op jit(solution)/shard_map/flash/pallas_call | solution.py:40
  31.8 1.3 %collective-permute-start.12 = (bf16[4,2,128,128]{3,2,1,0:T(8,128)(2,1)S(1)}, bf16[4,2,128,128]{3,2,1,0:T(8,128)(2,1)S(1)}, u32[]{:S(2)}, u32[]{:S(2)}) collective-permute-start(bf16[4,2,128,128]{3,2,1,0:T(8,128)(2,1)S(1)} %tie.5.refs_7_.refs_6_), channel_id=1, source_target_pairs={{16,24},{18,26},{20,28},{22,30},{17,25},{19,27},{21,29},{23,31}} | collective-permute-start | bytes 786440 | tf_op jit(solution)/shard_map/ppermute | solution.py:68
  33.3 1.6 %collective-permute-start.16 = (f32[16,1024]{1,0:T(8,128)S(1)}, f32[16,1024]{1,0:T(8,128)S(1)}, u32[]{:S(2)}, u32[]{:S(2)}) collective-permute-start(f32[16,1024]{1,0:T(8,128)S(1)} %get-tuple-element.53), channel_id=1, source_target_pairs={{0,2},{2,0},{4,6},{6,4},{8,10},{10,8},{12,14},{14,12},{16,18},{18,... | collective-permute-start | bytes 196616 | tf_op jit(solution)/shard_map/ppermute | solution.py:62
  34.9 1.3 %collective-permute-start.17 = (f32[16,1024]{1,0:T(8,128)S(1)}, f32[16,1024]{1,0:T(8,128)S(1)}, u32[]{:S(2)}, u32[]{:S(2)}) collective-permute-start(f32[16,1024]{1,0:T(8,128)S(1)} %get-tuple-element.54), channel_id=1, source_target_pairs={{0,4},{2,6},{4,0},{6,2},{8,12},{10,14},{12,8},{14,10},{16,20},{18,... | collective-permute-start | bytes 196616 | tf_op jit(solution)/shard_map/ppermute | solution.py:62
  36.9 1.7 %flash.4 = (f32[4,512,256]{2,1,0:T(8,128)S(1)}, f32[4,512,128]{2,1,0:T(8,128)S(1)}) custom-call(bf16[176,512]{1,0:T(8,128)(2,1)S(1)} %get-tuple-element.31.refs_1_.refs_0_, bf16[176,512]{1,0:T(8,128)(2,1)S(1)} %collective-permute-done.1.refs_1_, bf16[176,512]{1,0:T(8,128)(2,1)S(1)} %collective-permute-done.2.refs_2_, ...), custom_call_target="tpu_custom_call" | custom-call | flops 536870912 | bytes 7274496 | tf_op jit(solution)/shard_map/flash/pallas_call | solution.py:40
  38.6 1.5 %collective-permute-done.12.refs_6_ = bf16[4,2,128,128]{3,2,1,0:T(8,128)(2,1)S(1)} collective-permute-done((bf16[4,2,128,128]{3,2,1,0:T(8,128)(2,1)S(1)}, bf16[4,2,128,128]{3,2,1,0:T(8,128)(2,1)S(1)}, u32[]{:S(2)}, u32[]{:S(2)}) %collective-permute-start.12) | collective-permute-done | bytes 262176 | tf_op jit(solution)/shard_map/ppermute | solution.py:68
  40.0 1.8 %flash.5 = (bf16[128,512]{1,0:T(8,128)(2,1)S(1)}, bf16[128,512]{1,0:T(8,128)(2,1)S(1)}, bf16[128,512]{1,0:T(8,128)(2,1)S(1)}, bf16[128,512]{1,0:T(8,128)(2,1)S(1)}) custom-call(bf16[176,512]{1,0:T(8,128)(2,1)S(1)} %get-tuple-element.31.refs_1_.refs_0_, bf16[176,512]{1,0:T(8,128)(2,1)S(1)} %collective-permute-done.1.refs_1_, ...), custom_call_target="tpu_custom_call" | custom-call | flops 536870912 | bytes 4653056 | tf_op jit(solution)/shard_map/flash/pallas_call | solution.py:40
  41.8 2.3 %collective-permute-start.13 = (bf16[128,512]{1,0:T(8,128)(2,1)S(1)}, bf16[128,512]{1,0:T(8,128)(2,1)S(1)}, u32[]{:S(2)}, u32[]{:S(2)}) collective-permute-start(bf16[128,512]{1,0:T(8,128)(2,1)S(1)} %get-tuple-element.48), channel_id=1, source_target_pairs={{0,6},{2,4},{4,2},{6,0},{8,14},{10,12},{12,10},{14,8},{16,22},{18,... | collective-permute-start | bytes 393224 | tf_op jit(solution)/shard_map/ppermute | solution.py:62
  46.0 1.2 %collective-permute-done.19.refs_3_ = f32[128,128]{1,0:T(8,128)S(1)} collective-permute-done((f32[128,128]{1,0:T(8,128)S(1)}, f32[128,128]{1,0:T(8,128)S(1)}, u32[]{:S(2)}, u32[]{:S(2)}) %collective-permute-start.19) | collective-permute-done | bytes 65568 | tf_op jit(solution)/shard_map/ppermute | solution.py:611
  47.2 1.4 %norm.1 = bf16[128,4096]{1,0:T(8,128)(2,1)} custom-call(f32[128,4096]{1,0:T(8,128)S(1)} %get-tuple-element.56.refs_0_, f32[1,4096]{1,0:T(1,128)S(1)} %bitcast.11, f32[128,128]{1,0:T(8,128)S(1)} %get-tuple-element.57.refs_2_, f32[128,128]{1,0:T(8,128)S(1)} %collective-permute-done.19.refs_3_), custom_call_target="tpu_custom_call" | custom-call | bytes 3293184 | tf_op jit(solution)/shard_map/norm/pallas_call | solution.py:40
  (54 shorter events, 9.9 us)
Async XLA Ops:
  2.7 4.4 %copy-start.3 = (bf16[128,2048]{1,0:T(8,128)(2,1)S(1)}, bf16[128,2048]{1,0:T(8,128)(2,1)}, u32[]{:S(2)}) copy-start(bf16[128,2048]{1,0:T(8,128)(2,1)} %refs_5_.1) | copy-start | bytes 1572868
  2.7 4.4 %copy-start.6 = (f32[64]{0:T(128)S(1)}, f32[64]{0:T(128)}, u32[]{:S(2)}) copy-start(f32[64]{0:T(128)} %param.18) | copy-start | bytes 772
  2.7 5.3 %copy-start.1 = (bf16[128,4096]{1,0:T(8,128)(2,1)S(1)}, bf16[128,4096]{1,0:T(8,128)(2,1)}, u32[]{:S(2)}) copy-start(bf16[128,4096]{1,0:T(8,128)(2,1)} %refs_1_.5) | copy-start | bytes 3145732
  2.8 5.3 %copy-start.8 = (f32[64]{0:T(128)S(1)}, f32[64]{0:T(128)}, u32[]{:S(2)}) copy-start(f32[64]{0:T(128)} %param.20) | copy-start | bytes 772
  3.5 3.6 %collective-permute-start = (f32[128,256]{1,0:T(8,128)S(1)}, f32[128,256]{1,0:T(8,128)S(1)}, u32[]{:S(2)}, u32[]{:S(2)}) collective-permute-start(f32[128,256]{1,0:T(8,128)S(1)} %project.1.refs_0_), channel_id=1, source_target_pairs={{0,1},{1,0},{2,3},{3,2},{4,5},{5,4},{6,7},{7,6},{8,9},{9,8},{10,11... | collective-permute-start | bytes 393224 | tf_op jit(solution)/shard_map/ppermute | solution.py:611
  3.6 6.8 %collective-permute-start.4 = (bf16[2,128,128]{2,1,0:T(8,128)(2,1)S(1)}, bf16[2,128,128]{2,1,0:T(8,128)(2,1)S(1)}, u32[]{:S(2)}, u32[]{:S(2)}) collective-permute-start(bf16[2,128,128]{2,1,0:T(8,128)(2,1)S(1)} %get-tuple-element.40), channel_id=1, source_target_pairs={{0,2},{2,0},{4,6},{6,4},{8,10},{10,8},{12,14},{14,12},{16,18},{18,... | collective-permute-start | bytes 196616 | tf_op jit(solution)/shard_map/ppermute | solution.py:62
  5.1 5.2 %collective-permute-start.5 = (bf16[2,128,128]{2,1,0:T(8,128)(2,1)S(1)}, bf16[2,128,128]{2,1,0:T(8,128)(2,1)S(1)}, u32[]{:S(2)}, u32[]{:S(2)}) collective-permute-start(bf16[2,128,128]{2,1,0:T(8,128)(2,1)S(1)} %get-tuple-element.41), channel_id=1, source_target_pairs={{0,4},{2,6},{4,0},{6,2},{8,12},{10,14},{12,8},{14,10},{16,20},{18,... | collective-permute-start | bytes 196616 | tf_op jit(solution)/shard_map/ppermute | solution.py:62
  6.6 5.2 %collective-permute-start.6 = (bf16[2,128,128]{2,1,0:T(8,128)(2,1)S(1)}, bf16[2,128,128]{2,1,0:T(8,128)(2,1)S(1)}, u32[]{:S(2)}, u32[]{:S(2)}) collective-permute-start(bf16[2,128,128]{2,1,0:T(8,128)(2,1)S(1)} %get-tuple-element.42), channel_id=1, source_target_pairs={{0,6},{2,4},{4,2},{6,0},{8,14},{10,12},{12,10},{14,8},{16,22},{18,... | collective-permute-start | bytes 196616 | tf_op jit(solution)/shard_map/ppermute | solution.py:62
  11.8 8.8 %collective-permute-start.7 = (bf16[4,2,128,128]{3,2,1,0:T(8,128)(2,1)S(1)}, bf16[4,2,128,128]{3,2,1,0:T(8,128)(2,1)S(1)}, u32[]{:S(2)}, u32[]{:S(2)}) collective-permute-start(bf16[4,2,128,128]{3,2,1,0:T(8,128)(2,1)S(1)} %pad_maximum_fusion.refs_4_), channel_id=1, source_target_pairs={{0,8},{2,10},{4,12},{6,14},{8,16},{10,18},{12,20},{14,22},{16,24},... | collective-permute-start | bytes 786440 | tf_op jit(solution)/shard_map/ppermute | solution.py:68
  13.1 8.8 %collective-permute-start.1 = (bf16[176,512]{1,0:T(8,128)(2,1)S(1)}, bf16[176,512]{1,0:T(8,128)(2,1)S(1)}, u32[]{:S(2)}, u32[]{:S(2)}) collective-permute-start(bf16[176,512]{1,0:T(8,128)(2,1)S(1)} %get-tuple-element.32), channel_id=1, source_target_pairs={{0,2},{2,0},{4,6},{6,4},{8,10},{10,8},{12,14},{14,12},{16,18},{18,... | collective-permute-start | bytes 540680 | tf_op jit(solution)/shard_map/ppermute | solution.py:62
  13.7 9.4 %collective-permute-start.2 = (bf16[176,512]{1,0:T(8,128)(2,1)S(1)}, bf16[176,512]{1,0:T(8,128)(2,1)S(1)}, u32[]{:S(2)}, u32[]{:S(2)}) collective-permute-start(bf16[176,512]{1,0:T(8,128)(2,1)S(1)} %get-tuple-element.33), channel_id=1, source_target_pairs={{0,4},{2,6},{4,0},{6,2},{8,12},{10,14},{12,8},{14,10},{16,20},{18,... | collective-permute-start | bytes 540680 | tf_op jit(solution)/shard_map/ppermute | solution.py:62
  14.8 8.3 %collective-permute-start.3 = (bf16[176,512]{1,0:T(8,128)(2,1)S(1)}, bf16[176,512]{1,0:T(8,128)(2,1)S(1)}, u32[]{:S(2)}, u32[]{:S(2)}) collective-permute-start(bf16[176,512]{1,0:T(8,128)(2,1)S(1)} %get-tuple-element.34), channel_id=1, source_target_pairs={{0,6},{2,4},{4,2},{6,0},{8,14},{10,12},{12,10},{14,8},{16,22},{18,... | collective-permute-start | bytes 540680 | tf_op jit(solution)/shard_map/ppermute | solution.py:62
  20.7 11.1 %collective-permute-start.8 = (bf16[4,2,128,128]{3,2,1,0:T(8,128)(2,1)S(1)}, bf16[4,2,128,128]{3,2,1,0:T(8,128)(2,1)S(1)}, u32[]{:S(2)}, u32[]{:S(2)}) collective-permute-start(bf16[4,2,128,128]{3,2,1,0:T(8,128)(2,1)S(1)} %tie.4.refs_4_.refs_5_), channel_id=1, source_target_pairs={{8,16},{10,18},{12,20},{14,22},{16,24},{18,26},{20,28},{22,30},{9,... | collective-permute-start | bytes 786440 | tf_op jit(solution)/shard_map/ppermute | solution.py:68
  23.3 7.7 %collective-permute-start.10 = (bf16[16,1152]{1,0:T(8,128)(2,1)S(1)}, bf16[16,1152]{1,0:T(8,128)(2,1)S(1)}, u32[]{:S(2)}, u32[]{:S(2)}) collective-permute-start(bf16[16,1152]{1,0:T(8,128)(2,1)S(1)} %group_total.1.refs_6_), channel_id=1, source_target_pairs={{0,24},{2,26},{4,28},{6,30},{1,25},{3,27},{5,29},{7,31}} | collective-permute-start | bytes 110600 | tf_op jit(solution)/shard_map/ppermute | solution.py:68
  24.6 6.8 %collective-permute-start.11 = (bf16[16,1152]{1,0:T(8,128)(2,1)S(1)}, bf16[16,1152]{1,0:T(8,128)(2,1)S(1)}, u32[]{:S(2)}, u32[]{:S(2)}) collective-permute-start(bf16[16,1152]{1,0:T(8,128)(2,1)S(1)} %group_total.1.refs_6_), channel_id=1, source_target_pairs={{0,16},{2,18},{4,20},{6,22},{8,24},{10,26},{12,28},{14,30},{1,17},... | collective-permute-start | bytes 110600 | tf_op jit(solution)/shard_map/ppermute | solution.py:68
  25.9 5.9 %collective-permute-start.9 = (bf16[16,1152]{1,0:T(8,128)(2,1)S(1)}, bf16[16,1152]{1,0:T(8,128)(2,1)S(1)}, u32[]{:S(2)}, u32[]{:S(2)}) collective-permute-start(bf16[16,1152]{1,0:T(8,128)(2,1)S(1)} %group_total.1.refs_6_), channel_id=1, source_target_pairs={{0,8},{2,10},{4,12},{6,14},{8,16},{10,18},{12,20},{14,22},{16,24},... | collective-permute-start | bytes 110600 | tf_op jit(solution)/shard_map/ppermute | solution.py:68
  31.8 8.3 %collective-permute-start.12 = (bf16[4,2,128,128]{3,2,1,0:T(8,128)(2,1)S(1)}, bf16[4,2,128,128]{3,2,1,0:T(8,128)(2,1)S(1)}, u32[]{:S(2)}, u32[]{:S(2)}) collective-permute-start(bf16[4,2,128,128]{3,2,1,0:T(8,128)(2,1)S(1)} %tie.5.refs_7_.refs_6_), channel_id=1, source_target_pairs={{16,24},{18,26},{20,28},{22,30},{17,25},{19,27},{21,29},{23,31}} | collective-permute-start | bytes 786440 | tf_op jit(solution)/shard_map/ppermute | solution.py:68
  33.3 11.5 %collective-permute-start.16 = (f32[16,1024]{1,0:T(8,128)S(1)}, f32[16,1024]{1,0:T(8,128)S(1)}, u32[]{:S(2)}, u32[]{:S(2)}) collective-permute-start(f32[16,1024]{1,0:T(8,128)S(1)} %get-tuple-element.53), channel_id=1, source_target_pairs={{0,2},{2,0},{4,6},{6,4},{8,10},{10,8},{12,14},{14,12},{16,18},{18,... | collective-permute-start | bytes 196616 | tf_op jit(solution)/shard_map/ppermute | solution.py:62
  34.9 10.5 %collective-permute-start.17 = (f32[16,1024]{1,0:T(8,128)S(1)}, f32[16,1024]{1,0:T(8,128)S(1)}, u32[]{:S(2)}, u32[]{:S(2)}) collective-permute-start(f32[16,1024]{1,0:T(8,128)S(1)} %get-tuple-element.54), channel_id=1, source_target_pairs={{0,4},{2,6},{4,0},{6,2},{8,12},{10,14},{12,8},{14,10},{16,20},{18,... | collective-permute-start | bytes 196616 | tf_op jit(solution)/shard_map/ppermute | solution.py:62
  36.2 9.2 %collective-permute-start.18 = (f32[16,1024]{1,0:T(8,128)S(1)}, f32[16,1024]{1,0:T(8,128)S(1)}, u32[]{:S(2)}, u32[]{:S(2)}) collective-permute-start(f32[16,1024]{1,0:T(8,128)S(1)} %get-tuple-element.55), channel_id=1, source_target_pairs={{0,6},{2,4},{4,2},{6,0},{8,14},{10,12},{12,10},{14,8},{16,22},{18,... | collective-permute-start | bytes 196616 | tf_op jit(solution)/shard_map/ppermute | solution.py:62
  41.8 6.8 %collective-permute-start.13 = (bf16[128,512]{1,0:T(8,128)(2,1)S(1)}, bf16[128,512]{1,0:T(8,128)(2,1)S(1)}, u32[]{:S(2)}, u32[]{:S(2)}) collective-permute-start(bf16[128,512]{1,0:T(8,128)(2,1)S(1)} %get-tuple-element.48), channel_id=1, source_target_pairs={{0,6},{2,4},{4,2},{6,0},{8,14},{10,12},{12,10},{14,8},{16,22},{18,... | collective-permute-start | bytes 393224 | tf_op jit(solution)/shard_map/ppermute | solution.py:62
  44.1 5.0 %collective-permute-start.14 = (bf16[128,512]{1,0:T(8,128)(2,1)S(1)}, bf16[128,512]{1,0:T(8,128)(2,1)S(1)}, u32[]{:S(2)}, u32[]{:S(2)}) collective-permute-start(bf16[128,512]{1,0:T(8,128)(2,1)S(1)} %get-tuple-element.49), channel_id=1, source_target_pairs={{0,4},{2,6},{4,0},{6,2},{8,12},{10,14},{12,8},{14,10},{16,20},{18,... | collective-permute-start | bytes 393224 | tf_op jit(solution)/shard_map/ppermute | solution.py:62
  44.9 5.0 %collective-permute-start.15 = (bf16[128,512]{1,0:T(8,128)(2,1)S(1)}, bf16[128,512]{1,0:T(8,128)(2,1)S(1)}, u32[]{:S(2)}, u32[]{:S(2)}) collective-permute-start(bf16[128,512]{1,0:T(8,128)(2,1)S(1)} %get-tuple-element.50), channel_id=1, source_target_pairs={{0,2},{2,0},{4,6},{6,4},{8,10},{10,8},{12,14},{14,12},{16,18},{18,... | collective-permute-start | bytes 393224 | tf_op jit(solution)/shard_map/ppermute | solution.py:62
  45.9 1.3 %collective-permute-start.19 = (f32[128,128]{1,0:T(8,128)S(1)}, f32[128,128]{1,0:T(8,128)S(1)}, u32[]{:S(2)}, u32[]{:S(2)}) collective-permute-start(f32[128,128]{1,0:T(8,128)S(1)} %get-tuple-element.57.refs_2_), channel_id=1, source_target_pairs={{0,1},{1,0},{2,3},{3,2},{4,5},{5,4},{6,7},{7,6},{8,9},{9,8},{10,11... | collective-permute-start | bytes 196616 | tf_op jit(solution)/shard_map/ppermute | solution.py:611
  (7 other events, 14.5 us)
where the time goes:
time: 50.9 us; the launch traced here: 50.6 us
  starting transfers between devices  22.1 us (43%)
  Pallas kernels  13.9 us (27%)
  waiting for transfers between devices  11.6 us (23%)
  local copies, waits for them, and re-layouts  2 us (4%)
  between operations  0.94 us (2%)
    ppermute x12, starting transfers between devices, swap(): result[k] = lax.ppermute(pieces[k], 'ctx', perm)  14.2 us
    pallas_call x12, Pallas kernels, launch(): pl.pallas_call(body, **{} if grid is None else {'grid': grid}, out_shape=...  13.9 us
    ppermute x6, starting transfers between devices, climb_up(): return lax.ppermute(array, 'ctx', perm)  7.73 us
    ppermute x6, waiting for transfers between devices, climb_up(): return lax.ppermute(array, 'ctx', perm)  6.57 us
    ppermute x12, waiting for transfers between devices, swap(): result[k] = lax.ppermute(pieces[k], 'ctx', perm)  3.83 us
    unnamed x22, local copies, waits for them, and re-layouts  2 us
    ppermute x2, waiting for transfers between devices, shared_parts(): return [part, lax.ppermute(part, 'tp', [(0, 1), (1, 0)])]  1.24 us
  transfers between devices with their start and end apart: 20, of which 10 were waited for; matrix products, arithmetic and copies ran while one was open for 0% of the time, Pallas kernels for 24%

commit v1 on v0

--- a/solution.py
+++ b/solution.py
@@ -659,7 +659,7 @@
     still, scale = local_part(
         mixer_input, gate, climb, climb_t, step_t, maps, skip_gain[None], states
     )
-    own = jnp.stack([tie(blocks[0], [still])] + blocks[1:])
+    own = jnp.stack([tie(blocks[0], [climb])] + blocks[1:])
     sent = payloads[:1]
     payloads = swap(payloads, group, count)
     ring = 1 < turns <= UNROLL
@@ -667,7 +667,7 @@
     if ring:
         arrived.append(climb_up(own, group, count))
     if ring and turns > 2:
-        arrived[0] = tie(arrived[0], sent)
+        arrived[0] = tie(arrived[0], list(sent) + [still])
         ready = [arrived[0]]
         arrived.append(climb_up(arrived[0], group, count, first=1))
     total = group_total(payloads, length, states, width, after=ready)

time: 50.9 us -> 50.5 us (level)
    ppermute x6, waiting for transfers between devices: 6.57 us -> 4.66 us  [climb_up(): return lax.ppermute(array, 'ctx', perm)]
    ppermute x12, waiting for transfers between devices: 3.83 us -> 5.32 us  [swap(): result[k] = lax.ppermute(pieces[k], 'ctx', perm)]
  transfers between devices with their start and end apart: 20 -> 20, of which waited for: 10 -> 11; matrix products, arithmetic and copies ran while one was open for 0% -> 0% of each run, Pallas kernels for 24% -> 25%
where the time goes in v1:
time: 50.5 us; the launch traced here: 50.2 us
  starting transfers between devices  22.1 us (44%)
  Pallas kernels  14 us (28%)
  waiting for transfers between devices  11.2 us (22%)
  local copies, waits for them, and re-layouts  2 us (4%)
  between operations  0.91 us (2%)
    ppermute x12, starting transfers between devices, swap(): result[k] = lax.ppermute(pieces[k], 'ctx', perm)  14.2 us
    pallas_call x12, Pallas kernels, launch(): pl.pallas_call(body, **{} if grid is None else {'grid': grid}, out_shape=...  14 us
    ppermute x6, starting transfers between devices, climb_up(): return lax.ppermute(array, 'ctx', perm)  7.74 us
    ppermute x12, waiting for transfers between devices, swap(): result[k] = lax.ppermute(pieces[k], 'ctx', perm)  5.32 us
    ppermute x6, waiting for transfers between devices, climb_up(): return lax.ppermute(array, 'ctx', perm)  4.66 us
    unnamed x22, local copies, waits for them, and re-layouts  2 us
    ppermute x2, waiting for transfers between devices, shared_parts(): return [part, lax.ppermute(part, 'tp', [(0, 1), (1, 0)])]  1.24 us
  transfers between devices with their start and end apart: 20, of which 11 were waited for; matrix products, arithmetic and copies ran while one was open for 0% of the time, Pallas kernels for 25%

profile of v1, /device:TPU:24, one launch (start us, length us, event | category | flops | bytes accessed | tf_op | source)
XLA Modules:
  0.0 50.2 jit_solution(10891733676263099003)
XLA Ops:
  0.7 1.0 %copy-done.9 = bf16[128,512]{1,0:T(8,128)(2,1)S(1)} copy-done((bf16[128,512]{1,0:T(8,128)(2,1)S(1)}, bf16[128,512]{1,0:T(8,128)(2,1)}, u32[]{:S(2)}) %copy-start.9) | copy-done | bytes 131096
  3.6 1.6 %collective-permute-start.4 = (bf16[2,128,128]{2,1,0:T(8,128)(2,1)S(1)}, bf16[2,128,128]{2,1,0:T(8,128)(2,1)S(1)}, u32[]{:S(2)}, u32[]{:S(2)}) collective-permute-start(bf16[2,128,128]{2,1,0:T(8,128)(2,1)S(1)} %get-tuple-element.36), channel_id=1, source_target_pairs={{0,2},{2,0},{4,6},{6,4},{8,10},{10,8},{12,14},{14,12},{16,18},{18,... | collective-permute-start | bytes 196616 | tf_op jit(solution)/shard_map/ppermute | solution.py:62
  5.1 1.5 %collective-permute-start.5 = (bf16[2,128,128]{2,1,0:T(8,128)(2,1)S(1)}, bf16[2,128,128]{2,1,0:T(8,128)(2,1)S(1)}, u32[]{:S(2)}, u32[]{:S(2)}) collective-permute-start(bf16[2,128,128]{2,1,0:T(8,128)(2,1)S(1)} %get-tuple-element.37), channel_id=1, source_target_pairs={{0,4},{2,6},{4,0},{6,2},{8,12},{10,14},{12,8},{14,10},{16,20},{18,... | collective-permute-start | bytes 196616 | tf_op jit(solution)/shard_map/ppermute | solution.py:62
  8.1 1.3 %collective-permute-done.5 = bf16[2,128,128]{2,1,0:T(8,128)(2,1)S(1)} collective-permute-done((bf16[2,128,128]{2,1,0:T(8,128)(2,1)S(1)}, bf16[2,128,128]{2,1,0:T(8,128)(2,1)S(1)}, u32[]{:S(2)}, u32[]{:S(2)}) %collective-permute-start.5) | collective-permute-done | bytes 65568 | tf_op jit(solution)/shard_map/ppermute | solution.py:62
  9.4 2.4 %collective-permute-done.6 = bf16[2,128,128]{2,1,0:T(8,128)(2,1)S(1)} collective-permute-done((bf16[2,128,128]{2,1,0:T(8,128)(2,1)S(1)}, bf16[2,128,128]{2,1,0:T(8,128)(2,1)S(1)}, u32[]{:S(2)}, u32[]{:S(2)}) %collective-permute-start.6) | collective-permute-done | bytes 65568 | tf_op jit(solution)/shard_map/ppermute | solution.py:62
  11.8 1.3 %collective-permute-start.7 = (bf16[4,2,128,128]{3,2,1,0:T(8,128)(2,1)S(1)}, bf16[4,2,128,128]{3,2,1,0:T(8,128)(2,1)S(1)}, u32[]{:S(2)}, u32[]{:S(2)}) collective-permute-start(bf16[4,2,128,128]{3,2,1,0:T(8,128)(2,1)S(1)} %pad_maximum_fusion.refs_4_), channel_id=1, source_target_pairs={{0,8},{2,10},{4,12},{6,14},{8,16},{10,18},{12,20},{14,22},{16,24},... | collective-permute-start | bytes 786440 | tf_op jit(solution)/shard_map/ppermute | solution.py:68
  14.2 2.5 %collective-permute-start.3 = (bf16[176,512]{1,0:T(8,128)(2,1)S(1)}, bf16[176,512]{1,0:T(8,128)(2,1)S(1)}, u32[]{:S(2)}, u32[]{:S(2)}) collective-permute-start(bf16[176,512]{1,0:T(8,128)(2,1)S(1)} %get-tuple-element.34), channel_id=1, source_target_pairs={{0,6},{2,4},{4,2},{6,0},{8,14},{10,12},{12,10},{14,8},{16,22},{18,... | collective-permute-start | bytes 540680 | tf_op jit(solution)/shard_map/ppermute | solution.py:62
  16.7 2.3 %local_part.1 = (f32[128,4096]{1,0:T(8,128)S(1)}, f32[128,4096]{1,0:T(8,128)S(1)}) custom-call(bf16[128,4096]{1,0:T(8,128)(2,1)S(1)} %copy-done, bf16[128,4096]{1,0:T(8,128)(2,1)S(1)} %copy-done.1, f32[128,128]{1,0:T(8,128)S(1)} %get-tuple-element.35.refs_1_.refs_2_, f32[64,128]{1,0:T(8,128)S(1)} %get-tuple-element.39.refs_3_, ...), custom_call_target="tpu_custom_call" | custom-call | flops 268435456 | bytes 6488320 | tf_op jit(solution)/shard_map/local_part/pallas_call | solution.py:40
  19.0 1.7 %collective-permute-done.7.refs_0_ = bf16[4,2,128,128]{3,2,1,0:T(8,128)(2,1)S(1)} collective-permute-done((bf16[4,2,128,128]{3,2,1,0:T(8,128)(2,1)S(1)}, bf16[4,2,128,128]{3,2,1,0:T(8,128)(2,1)S(1)}, u32[]{:S(2)}, u32[]{:S(2)}) %collective-permute-start.7) | collective-permute-done | bytes 262176 | tf_op jit(solution)/shard_map/ppermute | solution.py:68
  20.7 1.3 %collective-permute-start.8 = (bf16[4,2,128,128]{3,2,1,0:T(8,128)(2,1)S(1)}, bf16[4,2,128,128]{3,2,1,0:T(8,128)(2,1)S(1)}, u32[]{:S(2)}, u32[]{:S(2)}) collective-permute-start(bf16[4,2,128,128]{3,2,1,0:T(8,128)(2,1)S(1)} %tie.4.refs_4_.refs_5_), channel_id=1, source_target_pairs={{8,16},{10,18},{12,20},{14,22},{16,24},{18,26},{20,28},{22,30},{9,... | collective-permute-start | bytes 786440 | tf_op jit(solution)/shard_map/ppermute | solution.py:68
  22.8 1.3 %collective-permute-start.10 = (bf16[16,1152]{1,0:T(8,128)(2,1)S(1)}, bf16[16,1152]{1,0:T(8,128)(2,1)S(1)}, u32[]{:S(2)}, u32[]{:S(2)}) collective-permute-start(bf16[16,1152]{1,0:T(8,128)(2,1)S(1)} %group_total.1.refs_6_), channel_id=1, source_target_pairs={{0,24},{2,26},{4,28},{6,30},{1,25},{3,27},{5,29},{7,31}} | collective-permute-start | bytes 110600 | tf_op jit(solution)/shard_map/ppermute | solution.py:68
  24.1 1.3 %collective-permute-start.11 = (bf16[16,1152]{1,0:T(8,128)(2,1)S(1)}, bf16[16,1152]{1,0:T(8,128)(2,1)S(1)}, u32[]{:S(2)}, u32[]{:S(2)}) collective-permute-start(bf16[16,1152]{1,0:T(8,128)(2,1)S(1)} %group_total.1.refs_6_), channel_id=1, source_target_pairs={{0,16},{2,18},{4,20},{6,22},{8,24},{10,26},{12,28},{14,30},{1,17},... | collective-permute-start | bytes 110600 | tf_op jit(solution)/shard_map/ppermute | solution.py:68
  25.4 1.3 %collective-permute-start.9 = (bf16[16,1152]{1,0:T(8,128)(2,1)S(1)}, bf16[16,1152]{1,0:T(8,128)(2,1)S(1)}, u32[]{:S(2)}, u32[]{:S(2)}) collective-permute-start(bf16[16,1152]{1,0:T(8,128)(2,1)S(1)} %group_total.1.refs_6_), channel_id=1, source_target_pairs={{0,8},{2,10},{4,12},{6,14},{8,16},{10,18},{12,20},{14,22},{16,24},... | collective-permute-start | bytes 110600 | tf_op jit(solution)/shard_map/ppermute | solution.py:68
  26.7 3.4 %flash.3 = (f32[4,512,256]{2,1,0:T(8,128)S(1)}, f32[4,512,128]{2,1,0:T(8,128)S(1)}) custom-call(bf16[176,512]{1,0:T(8,128)(2,1)S(1)} %get-tuple-element.31.refs_1_.refs_0_, bf16[176,512]{1,0:T(8,128)(2,1)S(1)} %collective-permute-done.1.refs_1_, bf16[176,512]{1,0:T(8,128)(2,1)S(1)} %collective-permute-done.2.refs_2_, ...), custom_call_target="tpu_custom_call" | custom-call | flops 1073741824 | bytes 4390912 | tf_op jit(solution)/shard_map/flash/pallas_call | solution.py:40
  31.6 1.3 %collective-permute-start.12 = (bf16[4,2,128,128]{3,2,1,0:T(8,128)(2,1)S(1)}, bf16[4,2,128,128]{3,2,1,0:T(8,128)(2,1)S(1)}, u32[]{:S(2)}, u32[]{:S(2)}) collective-permute-start(bf16[4,2,128,128]{3,2,1,0:T(8,128)(2,1)S(1)} %tie.5.refs_7_.refs_6_), channel_id=1, source_target_pairs={{16,24},{18,26},{20,28},{22,30},{17,25},{19,27},{21,29},{23,31}} | collective-permute-start | bytes 786440 | tf_op jit(solution)/shard_map/ppermute | solution.py:68
  33.2 1.3 %collective-permute-start.16 = (f32[16,1024]{1,0:T(8,128)S(1)}, f32[16,1024]{1,0:T(8,128)S(1)}, u32[]{:S(2)}, u32[]{:S(2)}) collective-permute-start(f32[16,1024]{1,0:T(8,128)S(1)} %get-tuple-element.53), channel_id=1, source_target_pairs={{0,2},{2,0},{4,6},{6,4},{8,10},{10,8},{12,14},{14,12},{16,18},{18,... | collective-permute-start | bytes 196616 | tf_op jit(solution)/shard_map/ppermute | solution.py:62
  35.2 1.5 %collective-permute-start.18 = (f32[16,1024]{1,0:T(8,128)S(1)}, f32[16,1024]{1,0:T(8,128)S(1)}, u32[]{:S(2)}, u32[]{:S(2)}) collective-permute-start(f32[16,1024]{1,0:T(8,128)S(1)} %get-tuple-element.55), channel_id=1, source_target_pairs={{0,6},{2,4},{4,2},{6,0},{8,14},{10,12},{12,10},{14,8},{16,22},{18,... | collective-permute-start | bytes 196616 | tf_op jit(solution)/shard_map/ppermute | solution.py:62
  36.7 1.7 %flash.4 = (f32[4,512,256]{2,1,0:T(8,128)S(1)}, f32[4,512,128]{2,1,0:T(8,128)S(1)}) custom-call(bf16[176,512]{1,0:T(8,128)(2,1)S(1)} %get-tuple-element.31.refs_1_.refs_0_, bf16[176,512]{1,0:T(8,128)(2,1)S(1)} %collective-permute-done.1.refs_1_, bf16[176,512]{1,0:T(8,128)(2,1)S(1)} %collective-permute-done.2.refs_2_, ...), custom_call_target="tpu_custom_call" | custom-call | flops 536870912 | bytes 7274496 | tf_op jit(solution)/shard_map/flash/pallas_call | solution.py:40
  38.5 1.4 %collective-permute-done.12.refs_6_ = bf16[4,2,128,128]{3,2,1,0:T(8,128)(2,1)S(1)} collective-permute-done((bf16[4,2,128,128]{3,2,1,0:T(8,128)(2,1)S(1)}, bf16[4,2,128,128]{3,2,1,0:T(8,128)(2,1)S(1)}, u32[]{:S(2)}, u32[]{:S(2)}) %collective-permute-start.12) | collective-permute-done | bytes 262176 | tf_op jit(solution)/shard_map/ppermute | solution.py:68
  39.9 1.8 %flash.5 = (bf16[128,512]{1,0:T(8,128)(2,1)S(1)}, bf16[128,512]{1,0:T(8,128)(2,1)S(1)}, bf16[128,512]{1,0:T(8,128)(2,1)S(1)}, bf16[128,512]{1,0:T(8,128)(2,1)S(1)}) custom-call(bf16[176,512]{1,0:T(8,128)(2,1)S(1)} %get-tuple-element.31.refs_1_.refs_0_, bf16[176,512]{1,0:T(8,128)(2,1)S(1)} %collective-permute-done.1.refs_1_, ...), custom_call_target="tpu_custom_call" | custom-call | flops 536870912 | bytes 4653056 | tf_op jit(solution)/shard_map/flash/pallas_call | solution.py:40
  41.7 1.4 %collective-permute-start.13 = (bf16[128,512]{1,0:T(8,128)(2,1)S(1)}, bf16[128,512]{1,0:T(8,128)(2,1)S(1)}, u32[]{:S(2)}, u32[]{:S(2)}) collective-permute-start(bf16[128,512]{1,0:T(8,128)(2,1)S(1)} %get-tuple-element.48), channel_id=1, source_target_pairs={{0,6},{2,4},{4,2},{6,0},{8,14},{10,12},{12,10},{14,8},{16,22},{18,... | collective-permute-start | bytes 393224 | tf_op jit(solution)/shard_map/ppermute | solution.py:62
  43.1 1.3 %collective-permute-start.14 = (bf16[128,512]{1,0:T(8,128)(2,1)S(1)}, bf16[128,512]{1,0:T(8,128)(2,1)S(1)}, u32[]{:S(2)}, u32[]{:S(2)}) collective-permute-start(bf16[128,512]{1,0:T(8,128)(2,1)S(1)} %get-tuple-element.49), channel_id=1, source_target_pairs={{0,4},{2,6},{4,0},{6,2},{8,12},{10,14},{12,8},{14,10},{16,20},{18,... | collective-permute-start | bytes 393224 | tf_op jit(solution)/shard_map/ppermute | solution.py:62
  45.9 1.2 %collective-permute-done.19.refs_3_ = f32[128,128]{1,0:T(8,128)S(1)} collective-permute-done((f32[128,128]{1,0:T(8,128)S(1)}, f32[128,128]{1,0:T(8,128)S(1)}, u32[]{:S(2)}, u32[]{:S(2)}) %collective-permute-start.19) | collective-permute-done | bytes 65568 | tf_op jit(solution)/shard_map/ppermute | solution.py:611
  47.1 1.4 %norm.1 = bf16[128,4096]{1,0:T(8,128)(2,1)} custom-call(f32[128,4096]{1,0:T(8,128)S(1)} %get-tuple-element.56.refs_0_, f32[1,4096]{1,0:T(1,128)S(1)} %bitcast.11, f32[128,128]{1,0:T(8,128)S(1)} %get-tuple-element.57.refs_2_, f32[128,128]{1,0:T(8,128)S(1)} %collective-permute-done.19.refs_3_), custom_call_target="tpu_custom_call" | custom-call | bytes 3293184 | tf_op jit(solution)/shard_map/norm/pallas_call | solution.py:40
  (54 shorter events, 10.7 us)
Async XLA Ops:
  2.7 4.4 %copy-start.3 = (bf16[128,2048]{1,0:T(8,128)(2,1)S(1)}, bf16[128,2048]{1,0:T(8,128)(2,1)}, u32[]{:S(2)}) copy-start(bf16[128,2048]{1,0:T(8,128)(2,1)} %refs_5_.1) | copy-start | bytes 1572868
  2.7 4.4 %copy-start.6 = (f32[64]{0:T(128)S(1)}, f32[64]{0:T(128)}, u32[]{:S(2)}) copy-start(f32[64]{0:T(128)} %param.18) | copy-start | bytes 772
  2.7 14.0 %copy-start.1 = (bf16[128,4096]{1,0:T(8,128)(2,1)S(1)}, bf16[128,4096]{1,0:T(8,128)(2,1)}, u32[]{:S(2)}) copy-start(bf16[128,4096]{1,0:T(8,128)(2,1)} %refs_1_.5) | copy-start | bytes 3145732
  2.8 13.9 %copy-start.8 = (f32[64]{0:T(128)S(1)}, f32[64]{0:T(128)}, u32[]{:S(2)}) copy-start(f32[64]{0:T(128)} %param.20) | copy-start | bytes 772
  3.5 3.6 %collective-permute-start = (f32[128,256]{1,0:T(8,128)S(1)}, f32[128,256]{1,0:T(8,128)S(1)}, u32[]{:S(2)}, u32[]{:S(2)}) collective-permute-start(f32[128,256]{1,0:T(8,128)S(1)} %project.1.refs_0_), channel_id=1, source_target_pairs={{0,1},{1,0},{2,3},{3,2},{4,5},{5,4},{6,7},{7,6},{8,9},{9,8},{10,11... | collective-permute-start | bytes 393224 | tf_op jit(solution)/shard_map/ppermute | solution.py:611
  3.6 4.5 %collective-permute-start.4 = (bf16[2,128,128]{2,1,0:T(8,128)(2,1)S(1)}, bf16[2,128,128]{2,1,0:T(8,128)(2,1)S(1)}, u32[]{:S(2)}, u32[]{:S(2)}) collective-permute-start(bf16[2,128,128]{2,1,0:T(8,128)(2,1)S(1)} %get-tuple-element.36), channel_id=1, source_target_pairs={{0,2},{2,0},{4,6},{6,4},{8,10},{10,8},{12,14},{14,12},{16,18},{18,... | collective-permute-start | bytes 196616 | tf_op jit(solution)/shard_map/ppermute | solution.py:62
  5.1 4.3 %collective-permute-start.5 = (bf16[2,128,128]{2,1,0:T(8,128)(2,1)S(1)}, bf16[2,128,128]{2,1,0:T(8,128)(2,1)S(1)}, u32[]{:S(2)}, u32[]{:S(2)}) collective-permute-start(bf16[2,128,128]{2,1,0:T(8,128)(2,1)S(1)} %get-tuple-element.37), channel_id=1, source_target_pairs={{0,4},{2,6},{4,0},{6,2},{8,12},{10,14},{12,8},{14,10},{16,20},{18,... | collective-permute-start | bytes 196616 | tf_op jit(solution)/shard_map/ppermute | solution.py:62
  6.6 5.2 %collective-permute-start.6 = (bf16[2,128,128]{2,1,0:T(8,128)(2,1)S(1)}, bf16[2,128,128]{2,1,0:T(8,128)(2,1)S(1)}, u32[]{:S(2)}, u32[]{:S(2)}) collective-permute-start(bf16[2,128,128]{2,1,0:T(8,128)(2,1)S(1)} %get-tuple-element.38), channel_id=1, source_target_pairs={{0,6},{2,4},{4,2},{6,0},{8,14},{10,12},{12,10},{14,8},{16,22},{18,... | collective-permute-start | bytes 196616 | tf_op jit(solution)/shard_map/ppermute | solution.py:62
  11.8 8.8 %collective-permute-start.7 = (bf16[4,2,128,128]{3,2,1,0:T(8,128)(2,1)S(1)}, bf16[4,2,128,128]{3,2,1,0:T(8,128)(2,1)S(1)}, u32[]{:S(2)}, u32[]{:S(2)}) collective-permute-start(bf16[4,2,128,128]{3,2,1,0:T(8,128)(2,1)S(1)} %pad_maximum_fusion.refs_4_), channel_id=1, source_target_pairs={{0,8},{2,10},{4,12},{6,14},{8,16},{10,18},{12,20},{14,22},{16,24},... | collective-permute-start | bytes 786440 | tf_op jit(solution)/shard_map/ppermute | solution.py:68
  13.1 8.8 %collective-permute-start.1 = (bf16[176,512]{1,0:T(8,128)(2,1)S(1)}, bf16[176,512]{1,0:T(8,128)(2,1)S(1)}, u32[]{:S(2)}, u32[]{:S(2)}) collective-permute-start(bf16[176,512]{1,0:T(8,128)(2,1)S(1)} %get-tuple-element.32), channel_id=1, source_target_pairs={{0,2},{2,0},{4,6},{6,4},{8,10},{10,8},{12,14},{14,12},{16,18},{18,... | collective-permute-start | bytes 540680 | tf_op jit(solution)/shard_map/ppermute | solution.py:62
  13.7 8.8 %collective-permute-start.2 = (bf16[176,512]{1,0:T(8,128)(2,1)S(1)}, bf16[176,512]{1,0:T(8,128)(2,1)S(1)}, u32[]{:S(2)}, u32[]{:S(2)}) collective-permute-start(bf16[176,512]{1,0:T(8,128)(2,1)S(1)} %get-tuple-element.33), channel_id=1, source_target_pairs={{0,4},{2,6},{4,0},{6,2},{8,12},{10,14},{12,8},{14,10},{16,20},{18,... | collective-permute-start | bytes 540680 | tf_op jit(solution)/shard_map/ppermute | solution.py:62
  14.2 8.3 %collective-permute-start.3 = (bf16[176,512]{1,0:T(8,128)(2,1)S(1)}, bf16[176,512]{1,0:T(8,128)(2,1)S(1)}, u32[]{:S(2)}, u32[]{:S(2)}) collective-permute-start(bf16[176,512]{1,0:T(8,128)(2,1)S(1)} %get-tuple-element.34), channel_id=1, source_target_pairs={{0,6},{2,4},{4,2},{6,0},{8,14},{10,12},{12,10},{14,8},{16,22},{18,... | collective-permute-start | bytes 540680 | tf_op jit(solution)/shard_map/ppermute | solution.py:62
  20.7 11.0 %collective-permute-start.8 = (bf16[4,2,128,128]{3,2,1,0:T(8,128)(2,1)S(1)}, bf16[4,2,128,128]{3,2,1,0:T(8,128)(2,1)S(1)}, u32[]{:S(2)}, u32[]{:S(2)}) collective-permute-start(bf16[4,2,128,128]{3,2,1,0:T(8,128)(2,1)S(1)} %tie.4.refs_4_.refs_5_), channel_id=1, source_target_pairs={{8,16},{10,18},{12,20},{14,22},{16,24},{18,26},{20,28},{22,30},{9,... | collective-permute-start | bytes 786440 | tf_op jit(solution)/shard_map/ppermute | solution.py:68
  22.8 8.0 %collective-permute-start.10 = (bf16[16,1152]{1,0:T(8,128)(2,1)S(1)}, bf16[16,1152]{1,0:T(8,128)(2,1)S(1)}, u32[]{:S(2)}, u32[]{:S(2)}) collective-permute-start(bf16[16,1152]{1,0:T(8,128)(2,1)S(1)} %group_total.1.refs_6_), channel_id=1, source_target_pairs={{0,24},{2,26},{4,28},{6,30},{1,25},{3,27},{5,29},{7,31}} | collective-permute-start | bytes 110600 | tf_op jit(solution)/shard_map/ppermute | solution.py:68
  24.1 7.5 %collective-permute-start.11 = (bf16[16,1152]{1,0:T(8,128)(2,1)S(1)}, bf16[16,1152]{1,0:T(8,128)(2,1)S(1)}, u32[]{:S(2)}, u32[]{:S(2)}) collective-permute-start(bf16[16,1152]{1,0:T(8,128)(2,1)S(1)} %group_total.1.refs_6_), channel_id=1, source_target_pairs={{0,16},{2,18},{4,20},{6,22},{8,24},{10,26},{12,28},{14,30},{1,17},... | collective-permute-start | bytes 110600 | tf_op jit(solution)/shard_map/ppermute | solution.py:68
  25.4 6.2 %collective-permute-start.9 = (bf16[16,1152]{1,0:T(8,128)(2,1)S(1)}, bf16[16,1152]{1,0:T(8,128)(2,1)S(1)}, u32[]{:S(2)}, u32[]{:S(2)}) collective-permute-start(bf16[16,1152]{1,0:T(8,128)(2,1)S(1)} %group_total.1.refs_6_), channel_id=1, source_target_pairs={{0,8},{2,10},{4,12},{6,14},{8,16},{10,18},{12,20},{14,22},{16,24},... | collective-permute-start | bytes 110600 | tf_op jit(solution)/shard_map/ppermute | solution.py:68
  31.6 8.3 %collective-permute-start.12 = (bf16[4,2,128,128]{3,2,1,0:T(8,128)(2,1)S(1)}, bf16[4,2,128,128]{3,2,1,0:T(8,128)(2,1)S(1)}, u32[]{:S(2)}, u32[]{:S(2)}) collective-permute-start(bf16[4,2,128,128]{3,2,1,0:T(8,128)(2,1)S(1)} %tie.5.refs_7_.refs_6_), channel_id=1, source_target_pairs={{16,24},{18,26},{20,28},{22,30},{17,25},{19,27},{21,29},{23,31}} | collective-permute-start | bytes 786440 | tf_op jit(solution)/shard_map/ppermute | solution.py:68
  33.2 11.2 %collective-permute-start.16 = (f32[16,1024]{1,0:T(8,128)S(1)}, f32[16,1024]{1,0:T(8,128)S(1)}, u32[]{:S(2)}, u32[]{:S(2)}) collective-permute-start(f32[16,1024]{1,0:T(8,128)S(1)} %get-tuple-element.53), channel_id=1, source_target_pairs={{0,2},{2,0},{4,6},{6,4},{8,10},{10,8},{12,14},{14,12},{16,18},{18,... | collective-permute-start | bytes 196616 | tf_op jit(solution)/shard_map/ppermute | solution.py:62
  34.5 10.8 %collective-permute-start.17 = (f32[16,1024]{1,0:T(8,128)S(1)}, f32[16,1024]{1,0:T(8,128)S(1)}, u32[]{:S(2)}, u32[]{:S(2)}) collective-permute-start(f32[16,1024]{1,0:T(8,128)S(1)} %get-tuple-element.54), channel_id=1, source_target_pairs={{0,4},{2,6},{4,0},{6,2},{8,12},{10,14},{12,8},{14,10},{16,20},{18,... | collective-permute-start | bytes 196616 | tf_op jit(solution)/shard_map/ppermute | solution.py:62
  35.2 10.1 %collective-permute-start.18 = (f32[16,1024]{1,0:T(8,128)S(1)}, f32[16,1024]{1,0:T(8,128)S(1)}, u32[]{:S(2)}, u32[]{:S(2)}) collective-permute-start(f32[16,1024]{1,0:T(8,128)S(1)} %get-tuple-element.55), channel_id=1, source_target_pairs={{0,6},{2,4},{4,2},{6,0},{8,14},{10,12},{12,10},{14,8},{16,22},{18,... | collective-permute-start | bytes 196616 | tf_op jit(solution)/shard_map/ppermute | solution.py:62
  41.7 6.8 %collective-permute-start.13 = (bf16[128,512]{1,0:T(8,128)(2,1)S(1)}, bf16[128,512]{1,0:T(8,128)(2,1)S(1)}, u32[]{:S(2)}, u32[]{:S(2)}) collective-permute-start(bf16[128,512]{1,0:T(8,128)(2,1)S(1)} %get-tuple-element.48), channel_id=1, source_target_pairs={{0,6},{2,4},{4,2},{6,0},{8,14},{10,12},{12,10},{14,8},{16,22},{18,... | collective-permute-start | bytes 393224 | tf_op jit(solution)/shard_map/ppermute | solution.py:62
  43.1 5.9 %collective-permute-start.14 = (bf16[128,512]{1,0:T(8,128)(2,1)S(1)}, bf16[128,512]{1,0:T(8,128)(2,1)S(1)}, u32[]{:S(2)}, u32[]{:S(2)}) collective-permute-start(bf16[128,512]{1,0:T(8,128)(2,1)S(1)} %get-tuple-element.49), channel_id=1, source_target_pairs={{0,4},{2,6},{4,0},{6,2},{8,12},{10,14},{12,8},{14,10},{16,20},{18,... | collective-permute-start | bytes 393224 | tf_op jit(solution)/shard_map/ppermute | solution.py:62
  44.4 5.0 %collective-permute-start.15 = (bf16[128,512]{1,0:T(8,128)(2,1)S(1)}, bf16[128,512]{1,0:T(8,128)(2,1)S(1)}, u32[]{:S(2)}, u32[]{:S(2)}) collective-permute-start(bf16[128,512]{1,0:T(8,128)(2,1)S(1)} %get-tuple-element.50), channel_id=1, source_target_pairs={{0,2},{2,0},{4,6},{6,4},{8,10},{10,8},{12,14},{14,12},{16,18},{18,... | collective-permute-start | bytes 393224 | tf_op jit(solution)/shard_map/ppermute | solution.py:62
  45.8 1.3 %collective-permute-start.19 = (f32[128,128]{1,0:T(8,128)S(1)}, f32[128,128]{1,0:T(8,128)S(1)}, u32[]{:S(2)}, u32[]{:S(2)}) collective-permute-start(f32[128,128]{1,0:T(8,128)S(1)} %get-tuple-element.57.refs_2_), channel_id=1, source_target_pairs={{0,1},{1,0},{2,3},{3,2},{4,5},{5,4},{6,7},{7,6},{8,9},{9,8},{10,11... | collective-permute-start | bytes 196616 | tf_op jit(solution)/shard_map/ppermute | solution.py:611
  (7 other events, 14.5 us)

commit v2 on v1

--- a/solution.py
+++ b/solution.py
@@ -173,16 +173,17 @@
             if n + 1 < len(tiles):
                 ahead = score(*tiles[n + 1])
             here = slice(start, start + tile)
-            top = jnp.broadcast_to(jnp.max(scores, axis=1, keepdims=True), (tile, LANES))
+            top = jnp.max(scores, axis=1, keepdims=True) * rate
+            top = jnp.broadcast_to(top, (tile, LANES))
             if not own:
                 top_before = before[1][h, here]
                 top = jnp.maximum(top_before, top)
             across = [top] * (rows // LANES)
             across = jnp.concatenate(across, axis=1) if len(across) > 1 else top
-            weights = jnp.exp2((scores - across) * rate).astype(BF16)
+            weights = jnp.exp2(scores * rate - across).astype(BF16)
             value = jnp.dot(weights, extended[...], preferred_element_type=F32)
             if not own:
-                keep = jnp.exp2((top_before - top) * rate)
+                keep = jnp.exp2(top_before - top)
                 value = value + before[0][h, here] * jnp.concatenate([keep, keep], axis=1)
             yield h, start, tile, value
             if after is not None:

time: 50.5 us -> 50.6 us (level)
  no operation moved by 1% of the time
where the time goes in v2:
time: 50.6 us; the launch traced here: 50.4 us
  starting transfers between devices  22.1 us (44%)
  Pallas kernels  14.3 us (28%)
  waiting for transfers between devices  10.9 us (22%)
  local copies, waits for them, and re-layouts  2 us (4%)
  between operations  1.07 us (2%)
    pallas_call x12, Pallas kernels, launch(): pl.pallas_call(body, **{} if grid is None else {'grid': grid}, out_shape=...  14.3 us
    ppermute x12, starting transfers between devices, swap(): result[k] = lax.ppermute(pieces[k], 'ctx', perm)  14.2 us
    ppermute x6, starting transfers between devices, climb_up(): return lax.ppermute(array, 'ctx', perm)  7.74 us
    ppermute x12, waiting for transfers between devices, swap(): result[k] = lax.ppermute(pieces[k], 'ctx', perm)  5.31 us
    ppermute x6, waiting for transfers between devices, climb_up(): return lax.ppermute(array, 'ctx', perm)  4.3 us
    unnamed x22, local copies, waits for them, and re-layouts  2 us
    ppermute x2, waiting for transfers between devices, shared_parts(): return [part, lax.ppermute(part, 'tp', [(0, 1), (1, 0)])]  1.24 us
  transfers between devices with their start and end apart: 20, of which 11 were waited for; matrix products, arithmetic and copies ran while one was open for 0% of the time, Pallas kernels for 25%

profile of v2, /device:TPU:24, one launch (start us, length us, event | category | flops | bytes accessed | tf_op | source)
XLA Modules:
  0.0 50.4 jit_solution(15686359364617311498)
XLA Ops:
  0.7 1.0 %copy-done.9 = bf16[128,512]{1,0:T(8,128)(2,1)S(1)} copy-done((bf16[128,512]{1,0:T(8,128)(2,1)S(1)}, bf16[128,512]{1,0:T(8,128)(2,1)}, u32[]{:S(2)}) %copy-start.9) | copy-done | bytes 131096
  3.6 1.6 %collective-permute-start.4 = (bf16[2,128,128]{2,1,0:T(8,128)(2,1)S(1)}, bf16[2,128,128]{2,1,0:T(8,128)(2,1)S(1)}, u32[]{:S(2)}, u32[]{:S(2)}) collective-permute-start(bf16[2,128,128]{2,1,0:T(8,128)(2,1)S(1)} %get-tuple-element.36), channel_id=1, source_target_pairs={{0,2},{2,0},{4,6},{6,4},{8,10},{10,8},{12,14},{14,12},{16,18},{18,... | collective-permute-start | bytes 196616 | tf_op jit(solution)/shard_map/ppermute | solution.py:62
  5.1 1.5 %collective-permute-start.5 = (bf16[2,128,128]{2,1,0:T(8,128)(2,1)S(1)}, bf16[2,128,128]{2,1,0:T(8,128)(2,1)S(1)}, u32[]{:S(2)}, u32[]{:S(2)}) collective-permute-start(bf16[2,128,128]{2,1,0:T(8,128)(2,1)S(1)} %get-tuple-element.37), channel_id=1, source_target_pairs={{0,4},{2,6},{4,0},{6,2},{8,12},{10,14},{12,8},{14,10},{16,20},{18,... | collective-permute-start | bytes 196616 | tf_op jit(solution)/shard_map/ppermute | solution.py:62
  8.1 1.3 %collective-permute-done.5 = bf16[2,128,128]{2,1,0:T(8,128)(2,1)S(1)} collective-permute-done((bf16[2,128,128]{2,1,0:T(8,128)(2,1)S(1)}, bf16[2,128,128]{2,1,0:T(8,128)(2,1)S(1)}, u32[]{:S(2)}, u32[]{:S(2)}) %collective-permute-start.5) | collective-permute-done | bytes 65568 | tf_op jit(solution)/shard_map/ppermute | solution.py:62
  9.4 2.4 %collective-permute-done.6 = bf16[2,128,128]{2,1,0:T(8,128)(2,1)S(1)} collective-permute-done((bf16[2,128,128]{2,1,0:T(8,128)(2,1)S(1)}, bf16[2,128,128]{2,1,0:T(8,128)(2,1)S(1)}, u32[]{:S(2)}, u32[]{:S(2)}) %collective-permute-start.6) | collective-permute-done | bytes 65568 | tf_op jit(solution)/shard_map/ppermute | solution.py:62
  11.8 1.3 %collective-permute-start.7 = (bf16[4,2,128,128]{3,2,1,0:T(8,128)(2,1)S(1)}, bf16[4,2,128,128]{3,2,1,0:T(8,128)(2,1)S(1)}, u32[]{:S(2)}, u32[]{:S(2)}) collective-permute-start(bf16[4,2,128,128]{3,2,1,0:T(8,128)(2,1)S(1)} %pad_maximum_fusion.refs_4_), channel_id=1, source_target_pairs={{0,8},{2,10},{4,12},{6,14},{8,16},{10,18},{12,20},{14,22},{16,24},... | collective-permute-start | bytes 786440 | tf_op jit(solution)/shard_map/ppermute | solution.py:68
  14.2 2.4 %collective-permute-start.3 = (bf16[176,512]{1,0:T(8,128)(2,1)S(1)}, bf16[176,512]{1,0:T(8,128)(2,1)S(1)}, u32[]{:S(2)}, u32[]{:S(2)}) collective-permute-start(bf16[176,512]{1,0:T(8,128)(2,1)S(1)} %get-tuple-element.34), channel_id=1, source_target_pairs={{0,6},{2,4},{4,2},{6,0},{8,14},{10,12},{12,10},{14,8},{16,22},{18,... | collective-permute-start | bytes 540680 | tf_op jit(solution)/shard_map/ppermute | solution.py:62
  16.7 2.3 %local_part.1 = (f32[128,4096]{1,0:T(8,128)S(1)}, f32[128,4096]{1,0:T(8,128)S(1)}) custom-call(bf16[128,4096]{1,0:T(8,128)(2,1)S(1)} %copy-done, bf16[128,4096]{1,0:T(8,128)(2,1)S(1)} %copy-done.1, f32[128,128]{1,0:T(8,128)S(1)} %get-tuple-element.35.refs_1_.refs_2_, f32[64,128]{1,0:T(8,128)S(1)} %get-tuple-element.39.refs_3_, ...), custom_call_target="tpu_custom_call" | custom-call | flops 268435456 | bytes 6488320 | tf_op jit(solution)/shard_map/local_part/pallas_call | solution.py:40
  19.0 1.7 %collective-permute-done.7.refs_0_ = bf16[4,2,128,128]{3,2,1,0:T(8,128)(2,1)S(1)} collective-permute-done((bf16[4,2,128,128]{3,2,1,0:T(8,128)(2,1)S(1)}, bf16[4,2,128,128]{3,2,1,0:T(8,128)(2,1)S(1)}, u32[]{:S(2)}, u32[]{:S(2)}) %collective-permute-start.7) | collective-permute-done | bytes 262176 | tf_op jit(solution)/shard_map/ppermute | solution.py:68
  20.7 1.3 %collective-permute-start.8 = (bf16[4,2,128,128]{3,2,1,0:T(8,128)(2,1)S(1)}, bf16[4,2,128,128]{3,2,1,0:T(8,128)(2,1)S(1)}, u32[]{:S(2)}, u32[]{:S(2)}) collective-permute-start(bf16[4,2,128,128]{3,2,1,0:T(8,128)(2,1)S(1)} %tie.4.refs_4_.refs_5_), channel_id=1, source_target_pairs={{8,16},{10,18},{12,20},{14,22},{16,24},{18,26},{20,28},{22,30},{9,... | collective-permute-start | bytes 786440 | tf_op jit(solution)/shard_map/ppermute | solution.py:68
  22.8 1.3 %collective-permute-start.10 = (bf16[16,1152]{1,0:T(8,128)(2,1)S(1)}, bf16[16,1152]{1,0:T(8,128)(2,1)S(1)}, u32[]{:S(2)}, u32[]{:S(2)}) collective-permute-start(bf16[16,1152]{1,0:T(8,128)(2,1)S(1)} %group_total.1.refs_6_), channel_id=1, source_target_pairs={{0,24},{2,26},{4,28},{6,30},{1,25},{3,27},{5,29},{7,31}} | collective-permute-start | bytes 110600 | tf_op jit(solution)/shard_map/ppermute | solution.py:68
  24.1 1.3 %collective-permute-start.11 = (bf16[16,1152]{1,0:T(8,128)(2,1)S(1)}, bf16[16,1152]{1,0:T(8,128)(2,1)S(1)}, u32[]{:S(2)}, u32[]{:S(2)}) collective-permute-start(bf16[16,1152]{1,0:T(8,128)(2,1)S(1)} %group_total.1.refs_6_), channel_id=1, source_target_pairs={{0,16},{2,18},{4,20},{6,22},{8,24},{10,26},{12,28},{14,30},{1,17},... | collective-permute-start | bytes 110600 | tf_op jit(solution)/shard_map/ppermute | solution.py:68
  25.4 1.3 %collective-permute-start.9 = (bf16[16,1152]{1,0:T(8,128)(2,1)S(1)}, bf16[16,1152]{1,0:T(8,128)(2,1)S(1)}, u32[]{:S(2)}, u32[]{:S(2)}) collective-permute-start(bf16[16,1152]{1,0:T(8,128)(2,1)S(1)} %group_total.1.refs_6_), channel_id=1, source_target_pairs={{0,8},{2,10},{4,12},{6,14},{8,16},{10,18},{12,20},{14,22},{16,24},... | collective-permute-start | bytes 110600 | tf_op jit(solution)/shard_map/ppermute | solution.py:68
  26.7 3.7 %flash.3 = (f32[4,512,256]{2,1,0:T(8,128)S(1)}, f32[4,512,128]{2,1,0:T(8,128)S(1)}) custom-call(bf16[176,512]{1,0:T(8,128)(2,1)S(1)} %get-tuple-element.31.refs_1_.refs_0_, bf16[176,512]{1,0:T(8,128)(2,1)S(1)} %collective-permute-done.1.refs_1_, bf16[176,512]{1,0:T(8,128)(2,1)S(1)} %collective-permute-done.2.refs_2_, ...), custom_call_target="tpu_custom_call" | custom-call | flops 1073741824 | bytes 4390912 | tf_op jit(solution)/shard_map/flash/pallas_call | solution.py:40
  31.6 1.3 %collective-permute-start.12 = (bf16[4,2,128,128]{3,2,1,0:T(8,128)(2,1)S(1)}, bf16[4,2,128,128]{3,2,1,0:T(8,128)(2,1)S(1)}, u32[]{:S(2)}, u32[]{:S(2)}) collective-permute-start(bf16[4,2,128,128]{3,2,1,0:T(8,128)(2,1)S(1)} %tie.5.refs_7_.refs_6_), channel_id=1, source_target_pairs={{16,24},{18,26},{20,28},{22,30},{17,25},{19,27},{21,29},{23,31}} | collective-permute-start | bytes 786440 | tf_op jit(solution)/shard_map/ppermute | solution.py:68
  33.2 1.3 %collective-permute-start.16 = (f32[16,1024]{1,0:T(8,128)S(1)}, f32[16,1024]{1,0:T(8,128)S(1)}, u32[]{:S(2)}, u32[]{:S(2)}) collective-permute-start(f32[16,1024]{1,0:T(8,128)S(1)} %get-tuple-element.53), channel_id=1, source_target_pairs={{0,2},{2,0},{4,6},{6,4},{8,10},{10,8},{12,14},{14,12},{16,18},{18,... | collective-permute-start | bytes 196616 | tf_op jit(solution)/shard_map/ppermute | solution.py:62
  35.2 1.5 %collective-permute-start.18 = (f32[16,1024]{1,0:T(8,128)S(1)}, f32[16,1024]{1,0:T(8,128)S(1)}, u32[]{:S(2)}, u32[]{:S(2)}) collective-permute-start(f32[16,1024]{1,0:T(8,128)S(1)} %get-tuple-element.55), channel_id=1, source_target_pairs={{0,6},{2,4},{4,2},{6,0},{8,14},{10,12},{12,10},{14,8},{16,22},{18,... | collective-permute-start | bytes 196616 | tf_op jit(solution)/shard_map/ppermute | solution.py:62
  36.7 1.8 %flash.4 = (f32[4,512,256]{2,1,0:T(8,128)S(1)}, f32[4,512,128]{2,1,0:T(8,128)S(1)}) custom-call(bf16[176,512]{1,0:T(8,128)(2,1)S(1)} %get-tuple-element.31.refs_1_.refs_0_, bf16[176,512]{1,0:T(8,128)(2,1)S(1)} %collective-permute-done.1.refs_1_, bf16[176,512]{1,0:T(8,128)(2,1)S(1)} %collective-permute-done.2.refs_2_, ...), custom_call_target="tpu_custom_call" | custom-call | flops 536870912 | bytes 7274496 | tf_op jit(solution)/shard_map/flash/pallas_call | solution.py:40
  38.6 1.3 %collective-permute-done.12.refs_6_ = bf16[4,2,128,128]{3,2,1,0:T(8,128)(2,1)S(1)} collective-permute-done((bf16[4,2,128,128]{3,2,1,0:T(8,128)(2,1)S(1)}, bf16[4,2,128,128]{3,2,1,0:T(8,128)(2,1)S(1)}, u32[]{:S(2)}, u32[]{:S(2)}) %collective-permute-start.12) | collective-permute-done | bytes 262176 | tf_op jit(solution)/shard_map/ppermute | solution.py:68
  39.9 1.8 %flash.5 = (bf16[128,512]{1,0:T(8,128)(2,1)S(1)}, bf16[128,512]{1,0:T(8,128)(2,1)S(1)}, bf16[128,512]{1,0:T(8,128)(2,1)S(1)}, bf16[128,512]{1,0:T(8,128)(2,1)S(1)}) custom-call(bf16[176,512]{1,0:T(8,128)(2,1)S(1)} %get-tuple-element.31.refs_1_.refs_0_, bf16[176,512]{1,0:T(8,128)(2,1)S(1)} %collective-permute-done.1.refs_1_, ...), custom_call_target="tpu_custom_call" | custom-call | flops 536870912 | bytes 4653056 | tf_op jit(solution)/shard_map/flash/pallas_call | solution.py:40
  41.7 1.4 %collective-permute-start.13 = (bf16[128,512]{1,0:T(8,128)(2,1)S(1)}, bf16[128,512]{1,0:T(8,128)(2,1)S(1)}, u32[]{:S(2)}, u32[]{:S(2)}) collective-permute-start(bf16[128,512]{1,0:T(8,128)(2,1)S(1)} %get-tuple-element.48), channel_id=1, source_target_pairs={{0,6},{2,4},{4,2},{6,0},{8,14},{10,12},{12,10},{14,8},{16,22},{18,... | collective-permute-start | bytes 393224 | tf_op jit(solution)/shard_map/ppermute | solution.py:62
  43.1 1.3 %collective-permute-start.14 = (bf16[128,512]{1,0:T(8,128)(2,1)S(1)}, bf16[128,512]{1,0:T(8,128)(2,1)S(1)}, u32[]{:S(2)}, u32[]{:S(2)}) collective-permute-start(bf16[128,512]{1,0:T(8,128)(2,1)S(1)} %get-tuple-element.49), channel_id=1, source_target_pairs={{0,4},{2,6},{4,0},{6,2},{8,12},{10,14},{12,8},{14,10},{16,20},{18,... | collective-permute-start | bytes 393224 | tf_op jit(solution)/shard_map/ppermute | solution.py:62
  45.9 1.2 %collective-permute-done.19.refs_3_ = f32[128,128]{1,0:T(8,128)S(1)} collective-permute-done((f32[128,128]{1,0:T(8,128)S(1)}, f32[128,128]{1,0:T(8,128)S(1)}, u32[]{:S(2)}, u32[]{:S(2)}) %collective-permute-start.19) | collective-permute-done | bytes 65568 | tf_op jit(solution)/shard_map/ppermute | solution.py:612
  47.1 1.4 %norm.1 = bf16[128,4096]{1,0:T(8,128)(2,1)} custom-call(f32[128,4096]{1,0:T(8,128)S(1)} %get-tuple-element.56.refs_0_, f32[1,4096]{1,0:T(1,128)S(1)} %bitcast.11, f32[128,128]{1,0:T(8,128)S(1)} %get-tuple-element.57.refs_2_, f32[128,128]{1,0:T(8,128)S(1)} %collective-permute-done.19.refs_3_), custom_call_target="tpu_custom_call" | custom-call | bytes 3293184 | tf_op jit(solution)/shard_map/norm/pallas_call | solution.py:40
  (54 shorter events, 10.5 us)
Async XLA Ops:
  2.7 4.4 %copy-start.3 = (bf16[128,2048]{1,0:T(8,128)(2,1)S(1)}, bf16[128,2048]{1,0:T(8,128)(2,1)}, u32[]{:S(2)}) copy-start(bf16[128,2048]{1,0:T(8,128)(2,1)} %refs_5_.1) | copy-start | bytes 1572868
  2.7 4.4 %copy-start.6 = (f32[64]{0:T(128)S(1)}, f32[64]{0:T(128)}, u32[]{:S(2)}) copy-start(f32[64]{0:T(128)} %param.18) | copy-start | bytes 772
  2.7 14.0 %copy-start.1 = (bf16[128,4096]{1,0:T(8,128)(2,1)S(1)}, bf16[128,4096]{1,0:T(8,128)(2,1)}, u32[]{:S(2)}) copy-start(bf16[128,4096]{1,0:T(8,128)(2,1)} %refs_1_.5) | copy-start | bytes 3145732
  2.8 13.9 %copy-start.8 = (f32[64]{0:T(128)S(1)}, f32[64]{0:T(128)}, u32[]{:S(2)}) copy-start(f32[64]{0:T(128)} %param.20) | copy-start | bytes 772
  3.5 3.6 %collective-permute-start = (f32[128,256]{1,0:T(8,128)S(1)}, f32[128,256]{1,0:T(8,128)S(1)}, u32[]{:S(2)}, u32[]{:S(2)}) collective-permute-start(f32[128,256]{1,0:T(8,128)S(1)} %project.1.refs_0_), channel_id=1, source_target_pairs={{0,1},{1,0},{2,3},{3,2},{4,5},{5,4},{6,7},{7,6},{8,9},{9,8},{10,11... | collective-permute-start | bytes 393224 | tf_op jit(solution)/shard_map/ppermute | solution.py:612
  3.6 4.5 %collective-permute-start.4 = (bf16[2,128,128]{2,1,0:T(8,128)(2,1)S(1)}, bf16[2,128,128]{2,1,0:T(8,128)(2,1)S(1)}, u32[]{:S(2)}, u32[]{:S(2)}) collective-permute-start(bf16[2,128,128]{2,1,0:T(8,128)(2,1)S(1)} %get-tuple-element.36), channel_id=1, source_target_pairs={{0,2},{2,0},{4,6},{6,4},{8,10},{10,8},{12,14},{14,12},{16,18},{18,... | collective-permute-start | bytes 196616 | tf_op jit(solution)/shard_map/ppermute | solution.py:62
  5.1 4.3 %collective-permute-start.5 = (bf16[2,128,128]{2,1,0:T(8,128)(2,1)S(1)}, bf16[2,128,128]{2,1,0:T(8,128)(2,1)S(1)}, u32[]{:S(2)}, u32[]{:S(2)}) collective-permute-start(bf16[2,128,128]{2,1,0:T(8,128)(2,1)S(1)} %get-tuple-element.37), channel_id=1, source_target_pairs={{0,4},{2,6},{4,0},{6,2},{8,12},{10,14},{12,8},{14,10},{16,20},{18,... | collective-permute-start | bytes 196616 | tf_op jit(solution)/shard_map/ppermute | solution.py:62
  6.6 5.2 %collective-permute-start.6 = (bf16[2,128,128]{2,1,0:T(8,128)(2,1)S(1)}, bf16[2,128,128]{2,1,0:T(8,128)(2,1)S(1)}, u32[]{:S(2)}, u32[]{:S(2)}) collective-permute-start(bf16[2,128,128]{2,1,0:T(8,128)(2,1)S(1)} %get-tuple-element.38), channel_id=1, source_target_pairs={{0,6},{2,4},{4,2},{6,0},{8,14},{10,12},{12,10},{14,8},{16,22},{18,... | collective-permute-start | bytes 196616 | tf_op jit(solution)/shard_map/ppermute | solution.py:62
  11.8 8.8 %collective-permute-start.7 = (bf16[4,2,128,128]{3,2,1,0:T(8,128)(2,1)S(1)}, bf16[4,2,128,128]{3,2,1,0:T(8,128)(2,1)S(1)}, u32[]{:S(2)}, u32[]{:S(2)}) collective-permute-start(bf16[4,2,128,128]{3,2,1,0:T(8,128)(2,1)S(1)} %pad_maximum_fusion.refs_4_), channel_id=1, source_target_pairs={{0,8},{2,10},{4,12},{6,14},{8,16},{10,18},{12,20},{14,22},{16,24},... | collective-permute-start | bytes 786440 | tf_op jit(solution)/shard_map/ppermute | solution.py:68
  13.1 8.8 %collective-permute-start.1 = (bf16[176,512]{1,0:T(8,128)(2,1)S(1)}, bf16[176,512]{1,0:T(8,128)(2,1)S(1)}, u32[]{:S(2)}, u32[]{:S(2)}) collective-permute-start(bf16[176,512]{1,0:T(8,128)(2,1)S(1)} %get-tuple-element.32), channel_id=1, source_target_pairs={{0,2},{2,0},{4,6},{6,4},{8,10},{10,8},{12,14},{14,12},{16,18},{18,... | collective-permute-start | bytes 540680 | tf_op jit(solution)/shard_map/ppermute | solution.py:62
  13.7 8.8 %collective-permute-start.2 = (bf16[176,512]{1,0:T(8,128)(2,1)S(1)}, bf16[176,512]{1,0:T(8,128)(2,1)S(1)}, u32[]{:S(2)}, u32[]{:S(2)}) collective-permute-start(bf16[176,512]{1,0:T(8,128)(2,1)S(1)} %get-tuple-element.33), channel_id=1, source_target_pairs={{0,4},{2,6},{4,0},{6,2},{8,12},{10,14},{12,8},{14,10},{16,20},{18,... | collective-permute-start | bytes 540680 | tf_op jit(solution)/shard_map/ppermute | solution.py:62
  14.2 8.3 %collective-permute-start.3 = (bf16[176,512]{1,0:T(8,128)(2,1)S(1)}, bf16[176,512]{1,0:T(8,128)(2,1)S(1)}, u32[]{:S(2)}, u32[]{:S(2)}) collective-permute-start(bf16[176,512]{1,0:T(8,128)(2,1)S(1)} %get-tuple-element.34), channel_id=1, source_target_pairs={{0,6},{2,4},{4,2},{6,0},{8,14},{10,12},{12,10},{14,8},{16,22},{18,... | collective-permute-start | bytes 540680 | tf_op jit(solution)/shard_map/ppermute | solution.py:62
  20.7 11.0 %collective-permute-start.8 = (bf16[4,2,128,128]{3,2,1,0:T(8,128)(2,1)S(1)}, bf16[4,2,128,128]{3,2,1,0:T(8,128)(2,1)S(1)}, u32[]{:S(2)}, u32[]{:S(2)}) collective-permute-start(bf16[4,2,128,128]{3,2,1,0:T(8,128)(2,1)S(1)} %tie.4.refs_4_.refs_5_), channel_id=1, source_target_pairs={{8,16},{10,18},{12,20},{14,22},{16,24},{18,26},{20,28},{22,30},{9,... | collective-permute-start | bytes 786440 | tf_op jit(solution)/shard_map/ppermute | solution.py:68
  22.8 8.0 %collective-permute-start.10 = (bf16[16,1152]{1,0:T(8,128)(2,1)S(1)}, bf16[16,1152]{1,0:T(8,128)(2,1)S(1)}, u32[]{:S(2)}, u32[]{:S(2)}) collective-permute-start(bf16[16,1152]{1,0:T(8,128)(2,1)S(1)} %group_total.1.refs_6_), channel_id=1, source_target_pairs={{0,24},{2,26},{4,28},{6,30},{1,25},{3,27},{5,29},{7,31}} | collective-permute-start | bytes 110600 | tf_op jit(solution)/shard_map/ppermute | solution.py:68
  24.1 7.5 %collective-permute-start.11 = (bf16[16,1152]{1,0:T(8,128)(2,1)S(1)}, bf16[16,1152]{1,0:T(8,128)(2,1)S(1)}, u32[]{:S(2)}, u32[]{:S(2)}) collective-permute-start(bf16[16,1152]{1,0:T(8,128)(2,1)S(1)} %group_total.1.refs_6_), channel_id=1, source_target_pairs={{0,16},{2,18},{4,20},{6,22},{8,24},{10,26},{12,28},{14,30},{1,17},... | collective-permute-start | bytes 110600 | tf_op jit(solution)/shard_map/ppermute | solution.py:68
  25.4 6.2 %collective-permute-start.9 = (bf16[16,1152]{1,0:T(8,128)(2,1)S(1)}, bf16[16,1152]{1,0:T(8,128)(2,1)S(1)}, u32[]{:S(2)}, u32[]{:S(2)}) collective-permute-start(bf16[16,1152]{1,0:T(8,128)(2,1)S(1)} %group_total.1.refs_6_), channel_id=1, source_target_pairs={{0,8},{2,10},{4,12},{6,14},{8,16},{10,18},{12,20},{14,22},{16,24},... | collective-permute-start | bytes 110600 | tf_op jit(solution)/shard_map/ppermute | solution.py:68
  31.6 8.3 %collective-permute-start.12 = (bf16[4,2,128,128]{3,2,1,0:T(8,128)(2,1)S(1)}, bf16[4,2,128,128]{3,2,1,0:T(8,128)(2,1)S(1)}, u32[]{:S(2)}, u32[]{:S(2)}) collective-permute-start(bf16[4,2,128,128]{3,2,1,0:T(8,128)(2,1)S(1)} %tie.5.refs_7_.refs_6_), channel_id=1, source_target_pairs={{16,24},{18,26},{20,28},{22,30},{17,25},{19,27},{21,29},{23,31}} | collective-permute-start | bytes 786440 | tf_op jit(solution)/shard_map/ppermute | solution.py:68
  33.2 11.3 %collective-permute-start.16 = (f32[16,1024]{1,0:T(8,128)S(1)}, f32[16,1024]{1,0:T(8,128)S(1)}, u32[]{:S(2)}, u32[]{:S(2)}) collective-permute-start(f32[16,1024]{1,0:T(8,128)S(1)} %get-tuple-element.53), channel_id=1, source_target_pairs={{0,2},{2,0},{4,6},{6,4},{8,10},{10,8},{12,14},{14,12},{16,18},{18,... | collective-permute-start | bytes 196616 | tf_op jit(solution)/shard_map/ppermute | solution.py:62
  34.5 10.8 %collective-permute-start.17 = (f32[16,1024]{1,0:T(8,128)S(1)}, f32[16,1024]{1,0:T(8,128)S(1)}, u32[]{:S(2)}, u32[]{:S(2)}) collective-permute-start(f32[16,1024]{1,0:T(8,128)S(1)} %get-tuple-element.54), channel_id=1, source_target_pairs={{0,4},{2,6},{4,0},{6,2},{8,12},{10,14},{12,8},{14,10},{16,20},{18,... | collective-permute-start | bytes 196616 | tf_op jit(solution)/shard_map/ppermute | solution.py:62
  35.2 10.1 %collective-permute-start.18 = (f32[16,1024]{1,0:T(8,128)S(1)}, f32[16,1024]{1,0:T(8,128)S(1)}, u32[]{:S(2)}, u32[]{:S(2)}) collective-permute-start(f32[16,1024]{1,0:T(8,128)S(1)} %get-tuple-element.55), channel_id=1, source_target_pairs={{0,6},{2,4},{4,2},{6,0},{8,14},{10,12},{12,10},{14,8},{16,22},{18,... | collective-permute-start | bytes 196616 | tf_op jit(solution)/shard_map/ppermute | solution.py:62
  41.7 6.8 %collective-permute-start.13 = (bf16[128,512]{1,0:T(8,128)(2,1)S(1)}, bf16[128,512]{1,0:T(8,128)(2,1)S(1)}, u32[]{:S(2)}, u32[]{:S(2)}) collective-permute-start(bf16[128,512]{1,0:T(8,128)(2,1)S(1)} %get-tuple-element.48), channel_id=1, source_target_pairs={{0,6},{2,4},{4,2},{6,0},{8,14},{10,12},{12,10},{14,8},{16,22},{18,... | collective-permute-start | bytes 393224 | tf_op jit(solution)/shard_map/ppermute | solution.py:62
  43.1 5.9 %collective-permute-start.14 = (bf16[128,512]{1,0:T(8,128)(2,1)S(1)}, bf16[128,512]{1,0:T(8,128)(2,1)S(1)}, u32[]{:S(2)}, u32[]{:S(2)}) collective-permute-start(bf16[128,512]{1,0:T(8,128)(2,1)S(1)} %get-tuple-element.49), channel_id=1, source_target_pairs={{0,4},{2,6},{4,0},{6,2},{8,12},{10,14},{12,8},{14,10},{16,20},{18,... | collective-permute-start | bytes 393224 | tf_op jit(solution)/shard_map/ppermute | solution.py:62
  44.5 5.0 %collective-permute-start.15 = (bf16[128,512]{1,0:T(8,128)(2,1)S(1)}, bf16[128,512]{1,0:T(8,128)(2,1)S(1)}, u32[]{:S(2)}, u32[]{:S(2)}) collective-permute-start(bf16[128,512]{1,0:T(8,128)(2,1)S(1)} %get-tuple-element.50), channel_id=1, source_target_pairs={{0,2},{2,0},{4,6},{6,4},{8,10},{10,8},{12,14},{14,12},{16,18},{18,... | collective-permute-start | bytes 393224 | tf_op jit(solution)/shard_map/ppermute | solution.py:62
  45.8 1.3 %collective-permute-start.19 = (f32[128,128]{1,0:T(8,128)S(1)}, f32[128,128]{1,0:T(8,128)S(1)}, u32[]{:S(2)}, u32[]{:S(2)}) collective-permute-start(f32[128,128]{1,0:T(8,128)S(1)} %get-tuple-element.57.refs_2_), channel_id=1, source_target_pairs={{0,1},{1,0},{2,3},{3,2},{4,5},{5,4},{6,7},{7,6},{8,9},{9,8},{10,11... | collective-permute-start | bytes 196616 | tf_op jit(solution)/shard_map/ppermute | solution.py:612
  (7 other events, 14.5 us)
